TPU v7x, 256 devices: a whole 4x4x8 slice. The times are simulated.
256 devices in a mesh: docs: 32 (over z_hi, x, core), heads: 8 (over z_lo, y).
Axes of the slice: x: 4, y: 4, z: 8 (z_hi: 4, z_lo: 2; z = z_hi * 2 + z_lo), core: 2. Of those that a mesh axis runs over, the one named last changes fastest.
Arguments:
- queries: bfloat16 [16384, 4096], P('docs', 'heads'), may hold values from -6 to 6
- keys: bfloat16 [16384, 2048], P('docs', 'heads'), may hold values from -6 to 6
- values: bfloat16 [16384, 2048], P('docs', 'heads'), may hold values from -6 to 6
- prefix_keys: bfloat16 [2048, 2048], P('docs', 'heads'), may hold values from -6 to 6
- prefix_values: bfloat16 [2048, 2048], P('docs', 'heads'), may hold values from -6 to 6
- out_grad: bfloat16 [16384, 4608], P('docs', 'heads'), may hold values from -24 to 24
- out_weight: bfloat16 [4096, 4608], P('heads'), may hold values from -0.09375 to 0.09375
- doc_lengths: int32 [32, 3], P('docs'), may hold values from 1 to 256, 512 in all within a row
Outputs:
- query_grad: bfloat16 [16384, 4096], P('docs', 'heads')
- key_grad: bfloat16 [16384, 2048], P('docs', 'heads')
- value_grad: bfloat16 [16384, 2048], P('docs', 'heads')
- prefix_key_grad: bfloat16 [2048, 2048], P('docs', 'heads')
- prefix_value_grad: bfloat16 [2048, 2048], P('docs', 'heads')
Inputs may be any that keep to these rules, and one draw needn't show every extreme that they name: Each row of doc_lengths sums to 512, and its largest entry is exactly 256.
All inputs are finite; a program needn't handle non-finite values.
Results may differ from a plain program's by a relative error of at most 0.02.
Values may be sent and summed in bfloat16 or wider, within the bound.
A program may use at most 128 MiB of HBM per device.

v0:
```python
import jax
import jax.numpy as jnp
from jax import lax
from jax.sharding import PartitionSpec as P

HEADS = 32
KV_HEADS = 16
HEAD_DIM = 128


softcap = 50.0
query_scale = 1.0 / 12.0


def doc_mask(lengths, count):
    bounds = jnp.cumsum(lengths)
    position = jnp.arange(count, dtype=jnp.int32)
    segment = jnp.sum((position[:, None] >= bounds[None, :]).astype(jnp.int32), axis=1)
    return (segment[:, None] == segment[None, :]) & (position[None, :] <= position[:, None])


def capped(raw):
    return softcap * jnp.tanh(raw * (query_scale / softcap))


def on_device(queries, keys, values, prefix_keys, prefix_values, out_grad, out_weight, doc_lengths):
    fl = jnp.float32
    tok = queries.shape[0]
    kv_local = keys.shape[1] // HEAD_DIM
    group = HEADS // KV_HEADS
    whole = lax.all_gather(out_grad, "heads", axis=1, tiled=True)
    head_grad = lax.dot_general(
        whole, out_weight, (((1,), (1,)), ((), ())), preferred_element_type=fl
    )
    head_grad = head_grad.astype(jnp.bfloat16)
    full_keys, full_values = (
        lax.all_gather(prefix_keys, "docs", axis=0, tiled=True),
        lax.all_gather(prefix_values, "docs", axis=0, tiled=True),
    )
    prefix_len = full_keys.shape[0]
    qrows = queries.reshape(tok, kv_local, group, HEAD_DIM)
    dout = head_grad.reshape(tok, kv_local, group, HEAD_DIM)
    krows = keys.reshape(tok, kv_local, HEAD_DIM)
    vrows = values.reshape(tok, kv_local, HEAD_DIM)
    pkrows = full_keys.reshape(prefix_len, kv_local, HEAD_DIM)
    pvrows = full_values.reshape(prefix_len, kv_local, HEAD_DIM)
    mask = doc_mask(doc_lengths[0], tok)
    s_pre = capped(jnp.einsum("tkgd,pkd->kgtp", qrows, pkrows, preferred_element_type=fl))
    s_doc = capped(jnp.einsum("tkgd,jkd->kgtj", qrows, krows, preferred_element_type=fl))
    e_pre = jnp.exp(s_pre)
    e_doc = jnp.where(mask, jnp.exp(s_doc), jnp.float32(0.0))
    total = jnp.sum(e_pre, axis=-1, keepdims=True) + jnp.sum(e_doc, axis=-1, keepdims=True)
    p_pre = e_pre / total
    p_doc = e_doc / total
    b_pre = p_pre.astype(jnp.bfloat16)
    b_doc = p_doc.astype(jnp.bfloat16)
    attn_out = jnp.einsum("kgtp,pkd->tkgd", b_pre, pvrows, preferred_element_type=fl) + jnp.einsum(
        "kgtj,jkd->tkgd", b_doc, vrows, preferred_element_type=fl
    )
    delta = jnp.sum(dout.astype(fl) * attn_out, axis=-1).transpose(1, 2, 0)[..., None]
    dp_pre = jnp.einsum("tkgd,pkd->kgtp", dout, pvrows, preferred_element_type=fl)
    dp_doc = jnp.einsum("tkgd,jkd->kgtj", dout, vrows, preferred_element_type=fl)
    l_pre = (
        p_pre * (dp_pre - delta) * (1.0 - s_pre / softcap * (s_pre / softcap)) * query_scale
    ).astype(jnp.bfloat16)
    l_doc = (
        p_doc * (dp_doc - delta) * (1.0 - s_doc / softcap * (s_doc / softcap)) * query_scale
    ).astype(jnp.bfloat16)
    dq = jnp.einsum("kgtp,pkd->tkgd", l_pre, pkrows, preferred_element_type=fl) + jnp.einsum(
        "kgtj,jkd->tkgd", l_doc, krows, preferred_element_type=fl
    )
    dk = jnp.einsum("kgtj,tkgd->jkd", l_doc, qrows, preferred_element_type=fl)
    dv = jnp.einsum("kgtj,tkgd->jkd", b_doc, dout, preferred_element_type=fl)
    query_grad = dq.reshape(tok, kv_local * group * HEAD_DIM).astype(jnp.bfloat16)
    key_grad = dk.reshape(tok, kv_local * HEAD_DIM).astype(jnp.bfloat16)
    value_grad = dv.reshape(tok, kv_local * HEAD_DIM).astype(jnp.bfloat16)
    owned = prefix_keys.shape[0]
    part = l_pre
    prefix_key_grad = lax.psum_scatter(
        jnp.einsum("kgtp,tkgd->pkd", part, qrows, preferred_element_type=fl)
        .reshape(owned * lax.axis_size("docs"), kv_local * HEAD_DIM)
        .astype(jnp.bfloat16),
        "docs",
        scatter_dimension=0,
        tiled=True,
    )
    part = b_pre
    prefix_value_grad = lax.psum_scatter(
        jnp.einsum("kgtp,tkgd->pkd", part, dout, preferred_element_type=fl)
        .reshape(owned * lax.axis_size("docs"), kv_local * HEAD_DIM)
        .astype(jnp.bfloat16),
        "docs",
        scatter_dimension=0,
        tiled=True,
    )
    return (query_grad, key_grad, value_grad, prefix_key_grad, prefix_value_grad)


def solution(mesh):
    return jax.shard_map(
        on_device,
        mesh=mesh,
        in_specs=(
            P("docs", "heads"),
            P("docs", "heads"),
            P("docs", "heads"),
            P("docs", "heads"),
            P("docs", "heads"),
            P("docs", "heads"),
            P("heads", None),
            P("docs", None),
        ),
        out_specs=(
            P("docs", "heads"),
            P("docs", "heads"),
            P("docs", "heads"),
            P("docs", "heads"),
            P("docs", "heads"),
        ),
        check_vma=False,
    )
```

profile of v0, /device:TPU:1, one launch (start us, length us, event | category | flops | bytes accessed | tf_op | source)
XLA Modules:
  0.0 388.0 jit_solution(477565676980357744)
XLA Ops:
  7.9 0.7 all-gather.8.cloned.1.call-update
  9.4 1.0 reshape.75
  10.6 1.8 reshape.78
  12.4 1.3 copy.163
  13.7 0.8 reduce-window.8
  14.8 3.4 fusion.8
  18.2 48.6 %all-gather.4.cloned.1.call-done = bf16[2048,256]{1,0:T(8,128)(2,1)} async-done(((bf16[64,256]{1,0:T(8,128)(2,1)}), bf16[2048,256]{1,0:T(8,128)(2,1)}) %all-gather.4.cloned.1.call-update) | async-done | bytes 1048592 | tf_op jit(solution)/shard_map/all_gather | solution.py:37
  66.8 1.5 copy.98
  68.3 8.1 %bitcast_reduce_fusion = (f32[2,2,512]{2,1,0:T(2,128)S(1)}, f32[2,2048,512,2]{2,1,3,0:T(8,128)}) fusion(bf16[2048,2,128,1]{0,2,3,1:T(8,128)(2,1)S(1)} %bitcast.140, bf16[512,2,2,128]{0,3,2,1:T(8,128)(2,1)S(1)} %bitcast.137), kind=kOutput, calls=%fused_computation.6 | convolution fusion | flops 1086322688 | bytes 18358272 | tf_op jit(solution)/shard_map/tkgd,pkd->kgtp/dot_general | solution.py:48
  76.4 42.5 %all-gather.8.cloned.1.call-done = bf16[2048,256]{1,0:T(8,128)(2,1)} async-done(((bf16[64,256]{1,0:T(8,128)(2,1)}), bf16[2048,256]{1,0:T(8,128)(2,1)}) %all-gather.8.cloned.1.call-update) | async-done | bytes 1048592 | tf_op jit(solution)/shard_map/all_gather | solution.py:38
  118.9 1.5 copy.103
  120.4 8.5 %fusion.3 = bf16[2,2,512,2048]{2,3,1,0:T(8,128)(2,1)S(1)} fusion(f32[2,2048,512,2]{2,1,3,0:T(8,128)} %get-tuple-element.26, f32[2,2,512]{2,1,0:T(2,128)S(1)} %add.22), kind=kLoop, calls=%fused_computation.9 | loop fusion | flops 16777216 | bytes 25174016 | tf_op jit(solution)/shard_map/convert_element_type | solution.py:55
  128.9 2.2 fusion.21
  131.1 2.4 copy-done
  133.5 0.7 copy-done.3
  134.2 1.3 fusion.11
  135.5 42.3 %all-gather.6.cloned.1.call-done = bf16[512,4608]{0,1:T(8,128)(2,1)} async-done(((bf16[512,576]{0,1:T(8,128)(2,1)}), bf16[512,4608]{0,1:T(8,128)(2,1)}) %all-gather.6.cloned.1.call-update) | async-done | bytes 4718608 | tf_op jit(solution)/shard_map/all_gather | solution.py:31
  177.8 6.5 %convolution_convert_fusion = bf16[512,512]{0,1:T(8,128)(2,1)S(1)} fusion(bf16[512,4608]{1,0:T(8,128)(2,1)} %param.14, bf16[512,4608]{0,1:T(8,128)(2,1)} %all-gather.6.cloned.1.call-done), kind=kOutput, calls=%fused_computation.28 | convolution fusion | flops 2416181248 | bytes 9961472 | tf_op jit(solution)/shard_map/dot_general | solution.py:32
  184.4 3.8 fusion.10
  188.7 13.2 %fusion.1 = bf16[2,2,512,2048]{2,3,1,0:T(8,128)(2,1)} fusion(f32[2,2048,512,2]{2,1,3,0:T(8,128)} %get-tuple-element.26, f32[2,2,512]{2,1,0:T(2,128)S(1)} %bitcast.152, f32[2,2,512]{2,1,0:T(2,128)S(1)} %add.22, bf16[512,2,2,128]{0,3,2,1:T(8,128)(2,1)S(1)} %bitcast.133, bf16[2048,2,128,1]{0,2,3,1:T(8,128)(2,1)S(1)} %bitcast.143), kind=kOutput, calls=%fused_computation.2 | convolution fusion | flops 1115684864 | bytes 26755072 | tf_op jit(solution)/shard_map/tkgd,pkd->kgtp/dot_general | solution.py:61
  201.9 2.3 copy.123
  204.4 7.2 %fusion.9 = bf16[2,2048,128]{1,2,0:T(8,128)(2,1)} fusion(bf16[2,2,512,2048]{2,3,1,0:T(8,128)(2,1)} %fusion.1, bf16[512,2,2,128]{0,3,2,1:T(8,128)(2,1)S(1)} %bitcast.138), kind=kOutput, calls=%fused_computation.21 | convolution fusion | flops 1074266112 | bytes 9961472 | tf_op jit(solution)/shard_map/kgtp,tkgd->pkd/dot_general | solution.py:80
  211.7 2.3 copy.121
  214.0 5.0 %fusion.5 = bf16[2,2,512,512]{2,3,1,0:T(8,128)(2,1)} fusion(f32[2,512,512,2]{2,1,3,0:T(8,128)} %get-tuple-element.28, bf16[512,2,2,128]{0,3,2,1:T(8,128)(2,1)S(1)} %bitcast.134, f32[2,2,512]{2,1,0:T(2,128)S(1)} %bitcast.153, f32[2,2,512]{2,1,0:T(2,128)S(1)} %add.22, pred[512,512]{0,1:T(8,128)(4,1)S(1)} %fusion.18, bf16[512,2,128,1]{2,1,0,3:T(2,128)(2,1)} %bitcast.150), kind=kOutput, calls=%fused_computation.12 | convolution fusion | flops 279969792 | bytes 7356416 | tf_op jit(solution)/shard_map/tkgd,jkd->kgtj/dot_general | solution.py:62
  219.0 0.8 fusion.17
  219.8 0.8 copy.126
  220.7 2.4 fusion.16
  223.1 0.8 copy.125
  223.9 5.2 %fusion.22 = f32[2,2,512,128]{2,3,1,0:T(8,128)S(1)} fusion(bf16[2048,2,128,1]{0,2,3,1:T(8,128)(2,1)} %bitcast.141, bf16[2,2,512,2048]{2,3,1,0:T(8,128)(2,1)} %fusion.1), kind=kOutput, calls=%fused_computation.42 | convolution fusion | flops 1073741824 | bytes 10485760 | tf_op jit(solution)/shard_map/kgtp,pkd->tkgd/dot_general | solution.py:69
  229.6 1.0 copy.124
  230.6 59.6 %reduce-scatter.5.cloned.1.call-done = bf16[64,256]{1,0:T(8,128)(2,1)} async-done(((bf16[2048,256]{1,0:T(8,128)(2,1)}), bf16[64,256]{1,0:T(8,128)(2,1)}) %reduce-scatter.5.cloned.1.call-update) | async-done | bytes 32784 | tf_op jit(solution)/shard_map/reduce_scatter | solution.py:88
  290.2 91.3 %reduce-scatter.3.cloned.1.call-done = bf16[64,256]{1,0:T(8,128)(2,1)} async-done(((bf16[2048,256]{1,0:T(8,128)(2,1)}), bf16[64,256]{1,0:T(8,128)(2,1)}) %reduce-scatter.3.cloned.1.call-update) | async-done | bytes 32784 | tf_op jit(solution)/shard_map/reduce_scatter | solution.py:79
  (35 shorter events, 3.3 us)
Async XLA Ops:
  7.2 59.7 %all-gather.4.cloned.1.call-start = ((), (), s32[]{:S(2)}) async-start(), calls=%async_computation.2 | async-start | bytes 1081344 | tf_op jit(solution)/shard_map/all_gather | solution.py:37
  7.9 111.0 %all-gather.8.cloned.1.call-start = ((), (), s32[]{:S(2)}) async-start(), calls=%async_computation.4 | async-start | bytes 1081344 | tf_op jit(solution)/shard_map/all_gather | solution.py:38
  8.6 169.2 %all-gather.6.cloned.1.call-start = ((), (), s32[]{:S(2)}) async-start(), calls=%async_computation.3 | async-start | bytes 5308416 | tf_op jit(solution)/shard_map/all_gather | solution.py:31
  9.4 280.8 %reduce-scatter.5.cloned.1.call-start = ((), (), s32[]{:S(2)}) async-start(), calls=%async_computation.6 | async-start | bytes 1081344 | tf_op jit(solution)/shard_map/reduce_scatter | solution.py:88
  10.6 7.6 %copy-start.8 = (bf16[512,2,128,1]{0,2,3,1:T(8,128)(2,1)}, bf16[512,2,128,1]{0,2,3,1:T(8,128)(2,1)S(1)}, u32[]{:S(2)}) copy-start(bf16[512,2,128,1]{0,2,3,1:T(8,128)(2,1)S(1)} %copy.142) | copy-start | bytes 786436
  68.3 8.1 %copy-start.4 = (bf16[2048,256]{0,1:T(8,128)(2,1)}, bf16[2048,256]{0,1:T(8,128)(2,1)S(1)}, u32[]{:S(2)}) copy-start(bf16[2048,256]{0,1:T(8,128)(2,1)S(1)} %copy.98) | copy-start | bytes 3145732
  120.4 8.5 %copy-start.5 = (bf16[2048,256]{0,1:T(8,128)(2,1)}, bf16[2048,256]{0,1:T(8,128)(2,1)S(1)}, u32[]{:S(2)}) copy-start(bf16[2048,256]{0,1:T(8,128)(2,1)S(1)} %copy.103) | copy-start | bytes 3145732
  128.9 4.7 %copy-start = (bf16[2,2,512,2048]{2,3,1,0:T(8,128)(2,1)}, bf16[2,2,512,2048]{2,3,1,0:T(8,128)(2,1)S(1)}, u32[]{:S(2)}) copy-start(bf16[2,2,512,2048]{2,3,1,0:T(8,128)(2,1)S(1)} %fusion.3) | copy-start | bytes 25165828
  128.9 5.3 %copy-start.3 = (f32[2,512,512,2]{2,1,3,0:T(8,128)S(1)}, f32[2,512,512,2]{2,1,3,0:T(8,128)}, u32[]{:S(2)}) copy-start(f32[2,512,512,2]{2,1,3,0:T(8,128)} %get-tuple-element.28) | copy-start | bytes 12582916
  177.8 6.5 %copy-start.1 = (bf16[2,2,512,2048]{2,3,1,0:T(8,128)(2,1)S(1)}, bf16[2,2,512,2048]{2,3,1,0:T(8,128)(2,1)}, u32[]{:S(2)}) copy-start(bf16[2,2,512,2048]{2,3,1,0:T(8,128)(2,1)} %copy-done) | copy-start | bytes 25165828
  184.3 3.8 copy-start.7
  184.4 3.8 copy-start.10
  184.4 4.3 %copy-start.6 = (bf16[2048,256]{0,1:T(8,128)(2,1)S(1)}, bf16[2048,256]{0,1:T(8,128)(2,1)}, u32[]{:S(2)}) copy-start(bf16[2048,256]{0,1:T(8,128)(2,1)} %copy-done.5) | copy-start | bytes 3145732
  204.2 177.3 %reduce-scatter.3.cloned.1.call-start = ((), (), s32[]{:S(2)}) async-start(), calls=%async_computation.5 | async-start | bytes 1081344 | tf_op jit(solution)/shard_map/reduce_scatter | solution.py:79
  223.9 5.2 %copy-start.2 = (bf16[2,2,512,512]{2,3,1,0:T(8,128)(2,1)S(1)}, bf16[2,2,512,512]{2,3,1,0:T(8,128)(2,1)}, u32[]{:S(2)}) copy-start(bf16[2,2,512,512]{2,3,1,0:T(8,128)(2,1)} %fusion.5) | copy-start | bytes 6291460
  223.9 5.2 %copy-start.9 = (bf16[512,2,128,1]{0,2,3,1:T(8,128)(2,1)S(1)}, bf16[512,2,128,1]{0,2,3,1:T(8,128)(2,1)}, u32[]{:S(2)}) copy-start(bf16[512,2,128,1]{0,2,3,1:T(8,128)(2,1)} %copy-done.8) | copy-start | bytes 786436
Sparse Core Ops, SparseCore 0:
  10.6 56.2 all-gather.3
  69.4 49.4 all-gather.7
  120.7 57.0 all-gather.5
  204.3 85.8 reduce-scatter.4
  294.8 86.5 reduce-scatter.2
where the time goes:
time: 389 us; the launch traced here: 388 us
  waiting for transfers between devices  286 us (74%)
  matrix products  58.8 us (15%)
  local copies, waits for them, and re-layouts  17.6 us (5%)
  between operations  14 us (4%)
  other arithmetic  10.9 us (3%)
    reduce_scatter x1, waiting for transfers between devices, on_device(): lax.psum_scatter(jnp.einsum('kgtp,tkgd->pkd', part, qrows, preferred_elem...  91.3 us
    reduce_scatter x1, waiting for transfers between devices, on_device(): lax.psum_scatter(jnp.einsum('kgtp,tkgd->pkd', part, dout, preferred_eleme...  59.6 us
    all_gather x1, waiting for transfers between devices, on_device(): lax.all_gather(prefix_keys, 'docs', axis=0, tiled=True)  48.6 us
    all_gather x1, waiting for transfers between devices, on_device(): lax.all_gather(prefix_values, 'docs', axis=0, tiled=True)  42.5 us
    all_gather x1, waiting for transfers between devices, on_device(): whole = lax.all_gather(out_grad, 'heads', axis=1, tiled=True)  42.3 us
    dot_general x1, matrix products, on_device(): jnp.einsum('tkgd,pkd->kgtp', dout, pvrows, preferred_element_type=fl)  13.2 us
    convert_element_type x1, other arithmetic, on_device(): b_pre = p_pre.astype(jnp.bfloat16)  8.47 us
    dot_general x1, matrix products, on_device(): jnp.einsum('tkgd,pkd->kgtp', qrows, pkrows, preferred_element_type=fl)  8.07 us
  transfers between devices with their start and end apart: 5, of which 5 were waited for; matrix products, arithmetic and copies ran while one was open for 15% of the time, Pallas kernels for 0%

commit v1 on v0

v1 whole, which is shorter than its diff:
```python
import functools
import math

import jax
import jax.numpy as jnp
from jax import lax
from jax.experimental import pallas as pl
from jax.experimental.pallas import tpu as pltpu
from jax.sharding import PartitionSpec as P

HD = 128
SOFTCAP = 50.0
SCALE = 1.0 / 12.0
LOG2E = 1.4426950408889634
F32 = jnp.float32
BF16 = jnp.bfloat16
MESH = pl.DeviceIdType.MESH

TOK = 512
FEAT = 576
NC = 4
CH = TOK // NC
QW = 1024
CW = 256


def dot(a, b, dims=((1,), (0,))):
    return lax.dot_general(a, b, (dims, ((), ())), preferred_element_type=F32)


def kernel(
    len_ref, q_ref, k_ref, v_ref, pk_ref, pv_ref, og_ref, w_ref,
    dq_ref, dk_ref, dv_ref, pdk_ref, pdv_ref,
    gbuf, wraw, wt, kbuf, vbuf, ebuf, sbuf, edoc, sdoc, qt, qs, dot_t, dos, dqt, ot, lsum, drow, hg,
    pb, pr, xs, xr, acc, zs, zr,
    w_sem, gs, gr, kzs, kzr, kxs, kxr, kcs, kcr, ps, prs, xss, xrs, zss, zrs,
):
    d = lax.axis_index("docs")
    h = lax.axis_index("heads")
    core = lax.rem(d, 2)
    x = lax.rem(d // 2, 4)
    zh = d // 8
    zl = h // 4
    y = lax.rem(h, 4)

    def doc_id(zz, xx, cc):
        return {"docs": (lax.rem(zz, 4) * 4 + lax.rem(xx, 4)) * 2 + cc}

    def head_at(zz, yy):
        return zz * 4 + lax.rem(yy + 8, 4)

    peers = [doc_id(zh + r, x, core) for r in (1, 2, 3)]
    peers += [doc_id(zh, x + r, core) for r in (1, 2, 3)]
    peers += [doc_id(zh, x, 1 - core)]
    peers += [{"heads": head_at(zl, y + 1)}, {"heads": head_at(zl, y - 1)}, {"heads": head_at(1 - zl, y)}]

    wcopy = pltpu.make_async_copy(w_ref, wraw, w_sem)
    wcopy.start()

    barrier = pltpu.get_barrier_semaphore()
    for p in peers:
        pl.semaphore_signal(barrier, inc=1, device_id=p, device_id_type=MESH)
    pl.semaphore_wait(barrier, len(peers))

    started = []

    def remote(src, dst, ssem, rsem, device):
        return pltpu.make_async_remote_copy(
            src_ref=src, dst_ref=dst, send_sem=ssem, recv_sem=rsem, device_id=device, device_id_type=MESH
        )

    def send(*args):
        c = remote(*args)
        c.start()
        started.append(c)

    def g_route(kind, c):
        s = 1 if c % 2 == 0 else -1
        right, left = y + s, y - s
        return [
            (head_at(zl, y), head_at(zl, right), head_at(zl, left)),
            (head_at(zl, y), head_at(zl, left), head_at(zl, right)),
            (head_at(zl, y), head_at(1 - zl, y), head_at(1 - zl, y)),
            (head_at(1 - zl, y), head_at(zl, right), head_at(1 - zl, left)),
            (head_at(zl, right), head_at(zl, left), head_at(zl, y + 2)),
            (head_at(zl, right), head_at(1 - zl, y), head_at(1 - zl, right)),
            (head_at(1 - zl, left), head_at(zl, right), head_at(1 - zl, y + 2)),
        ][kind]

    def g_copy(kind, c, receive):
        slot, to, arrives = g_route(kind, c)
        rows = pl.ds(c * CH, CH)
        at = gbuf.at[arrives if receive else slot, rows]
        src = og_ref.at[rows] if kind < 3 and not receive else at
        return remote(src, at, gs.at[kind, c], gr.at[kind, c], {"heads": to})

    def g_send(kind, c):
        cp = g_copy(kind, c, False)
        cp.start()
        started.append(cp)

    def g_wait(kind, c):
        g_copy(kind, c, True).wait_recv()

    both = ((0, pk_ref, kbuf), (1, pv_ref, vbuf))
    for i, src, buf in both:
        for r in (1, 2, 3):
            send(src, buf.at[zh, x, core], kzs.at[i, r - 1], kzr.at[i, r - 1], doc_id(zh + r, x, core))
    for c in range(NC):
        for kind in range(3):
            g_send(kind, c)
    for i, src, buf in both:
        buf[zh, x, core] = src[...]

    for hd in range(4):
        blk = q_ref[:, hd * HD : (hd + 1) * HD]
        qs[hd // 2, (hd % 2) * TOK : (hd % 2 + 1) * TOK, :] = blk
        qt[hd // 2, :, (hd % 2) * TOK : (hd % 2 + 1) * TOK] = blk.T
    ot[...] = jnp.zeros_like(ot)
    lsum[...] = jnp.zeros_like(lsum)

    def forward(kk, vv, hk, put, mask=None):
        rows = kk.shape[0]
        for n in range(QW // CW):
            cols = slice(n * CW, (n + 1) * CW)
            t = jnp.tanh(dot(kk, qt[hk, :, cols]) * (SCALE / SOFTCAP))
            e = jnp.exp2(t * (SOFTCAP * LOG2E))
            if mask is not None:
                e = jnp.where(mask(n * CW), e, 0.0)
            lsum[hk, :, cols] += jnp.sum(e.reshape(rows // 8, 8, CW), axis=0)
            eb = e.astype(BF16)
            put(cols, eb, (e * (1.0 - t * t)).astype(BF16))
            ot[hk, :, cols] += dot(vv, eb, ((0,), (0,)))

    b0 = len_ref[0, 0]
    b1 = b0 + len_ref[0, 1]
    b2 = b1 + len_ref[0, 2]

    def segment(p):
        return (p >= b0).astype(jnp.int32) + (p >= b1).astype(jnp.int32) + (p >= b2).astype(jnp.int32)

    def doc_forward(i, carry):
        hk = i // 4
        j = lax.rem(i, 4)
        rows = pl.ds(pl.multiple_of(j * HD, HD), HD)
        lanes = pl.ds(pl.multiple_of(hk * HD, HD), HD)

        def mask(first):
            key = j * HD + lax.broadcasted_iota(jnp.int32, (HD, CW), 0)
            row = first % TOK + lax.broadcasted_iota(jnp.int32, (HD, CW), 1)
            return (key <= row) & (segment(key) == segment(row))

        def put(cols, eb, sb):
            edoc[hk, rows, cols] = eb
            sdoc[hk, rows, cols] = sb

        forward(k_ref[rows, lanes], v_ref[rows, lanes], hk, put, mask)
        return carry

    lax.fori_loop(0, 8, doc_forward, 0)

    for i, src, buf in both:
        for r in (1, 2, 3):
            remote(src, buf.at[lax.rem(zh - r + 4, 4), x, core], kzs.at[i, r - 1], kzr.at[i, r - 1], doc_id(zh + r, x, core)).wait_recv()
        mine = buf.at[:, x, core]
        for r in (1, 2, 3):
            send(mine, mine, kxs.at[i, r - 1], kxr.at[i, r - 1], doc_id(zh, x + r, core))
        send(mine, mine, kcs.at[i, 0], kcr.at[i, 0], doc_id(zh, x, 1 - core))

    def g_forward(c):
        g_wait(2, c)
        g_send(3, c)
        g_wait(1, c)
        g_send(4, c)
        g_send(5, c)

    def g_last(c):
        g_wait(3, c)
        g_send(6, c)

    g_forward(0)
    g_forward(1)

    wcopy.wait()
    for i in range(4608 // HD):
        wt[i * HD : (i + 1) * HD, :] = wraw[:, i * HD : (i + 1) * HD].T

    g_forward(2)
    g_last(0)

    for i, src, buf in both:
        for r in (1, 2, 3):
            at = buf.at[:, lax.rem(x - r + 4, 4), core]
            remote(at, at, kxs.at[i, r - 1], kxr.at[i, r - 1], doc_id(zh, x + r, core)).wait_recv()
            send(at, at, kcs.at[i, r], kcr.at[i, r], doc_id(zh, x, 1 - core))
    g_forward(3)
    g_last(1)
    for i, src, buf in both:
        for r in range(4):
            at = buf.at[:, lax.rem(x - r + 4, 4), 1 - core]
            remote(at, at, kcs.at[i, r], kcr.at[i, r], doc_id(zh, x, 1 - core)).wait_recv()

    def pre_forward(i, carry):
        hk = i // 4
        zz = lax.rem(i, 4)
        lanes = pl.ds(pl.multiple_of(hk * HD, HD), HD)
        for xx in range(2):
            kk = kbuf[zz, 2 * xx : 2 * xx + 2, :, :, lanes].reshape(256, HD)
            vv = vbuf[zz, 2 * xx : 2 * xx + 2, :, :, lanes].reshape(256, HD)

            def put(cols, eb, sb):
                ebuf[hk, zz, 2 * xx : 2 * xx + 2, :, cols] = eb.reshape(2, HD, CW)
                sbuf[hk, zz, 2 * xx : 2 * xx + 2, :, cols] = sb.reshape(2, HD, CW)

            forward(kk, vv, hk, put)
        return carry

    lax.fori_loop(0, 4, pre_forward, 0)
    g_last(2)
    g_last(3)
    lax.fori_loop(4, 8, pre_forward, 0)

    def w_rows(s):
        return wt[pl.ds(pl.multiple_of(s * FEAT, FEAT), FEAT), :]

    hg[...] = dot(og_ref[...], w_rows(h))
    for kind, waited in ((0, False), (1, True), (2, True), (3, True), (5, False), (4, False), (6, False)):
        for c in range(NC):
            if not waited:
                g_wait(kind, c)
            slot = g_route(kind, c)[2]
            rows = slice(c * CH, (c + 1) * CH)
            hg[rows, :] += dot(gbuf[slot, rows, :], w_rows(slot))

    dqt[...] = jnp.zeros_like(dqt)
    for hd in range(4):
        hk, cols = hd // 2, slice((hd % 2) * TOK, (hd % 2 + 1) * TOK)
        g_t = hg[:, hd * HD : (hd + 1) * HD].T.astype(BF16).astype(F32)
        inv = 1.0 / jnp.sum(lsum[hk, :, cols], axis=0, keepdims=True)
        scaled = (g_t * inv).astype(BF16)
        drow[hk, :, cols] = jnp.sum(g_t * ot[hk, :, cols], axis=0, keepdims=True) * (inv * inv)
        dot_t[hk, :, cols] = scaled
        dos[hk, cols, :] = scaled.astype(F32).T.astype(BF16)

    def backward(kk, vv, hk, get):
        dk = dv = None
        for n in range(QW // CW):
            cols = slice(n * CW, (n + 1) * CW)
            eb, sb = get(cols)
            dp = dot(vv, dot_t[hk, :, cols]) - drow[hk, :, cols]
            ds = (sb.astype(F32) * dp).astype(BF16)
            a = dot(ds, qs[hk, cols, :])
            b = dot(eb, dos[hk, cols, :])
            dk = a if dk is None else dk + a
            dv = b if dv is None else dv + b
            dqt[hk, :, cols] += dot(kk, ds, ((0,), (0,)))
        return dk * SCALE, dv

    def quarter(r):
        xx = lax.rem(x + r, 4)

        def one(i, carry):
            hk = i // 2
            zz = lax.rem(i, 2) * 2
            lanes = pl.ds(pl.multiple_of(hk * HD, HD), HD)
            kk = kbuf[pl.ds(zz, 2), xx, :, :, lanes].reshape(256, HD)
            vv = vbuf[pl.ds(zz, 2), xx, :, :, lanes].reshape(256, HD)

            def get(cols):
                eb = ebuf[hk, pl.ds(zz, 2), xx, :, cols].reshape(256, CW)
                sb = sbuf[hk, pl.ds(zz, 2), xx, :, cols].reshape(256, CW)
                return eb, sb

            dk, dv = backward(kk, vv, hk, get)
            dk = dk.astype(BF16).reshape(2, 2, 64, HD)
            dv = dv.astype(BF16).reshape(2, 2, 64, HD)
            for cc in range(2):
                pb[r, cc, 0, pl.ds(zz, 2), :, lanes] = dk[:, cc]
                pb[r, cc, 1, pl.ds(zz, 2), :, lanes] = dv[:, cc]
            return carry

        lax.fori_loop(0, 4, one, 0)
        send(pb.at[r, 1 - core], pr.at[r], ps.at[r], prs.at[r], doc_id(zh, x, 1 - core))

    def pair_sum(r):
        remote(pb.at[r, 1 - core], pr.at[r], ps.at[r], prs.at[r], doc_id(zh, x, 1 - core)).wait_recv()
        return pb[r, core].astype(F32) + pr[r].astype(F32)

    def x_send(r):
        xs[r - 1] = pair_sum(r).astype(BF16)
        send(xs.at[r - 1], xr.at[r - 1], xss.at[r - 1], xrs.at[r - 1], doc_id(zh, x + r, core))

    quarter(2)
    quarter(1)
    x_send(2)
    quarter(3)
    x_send(1)
    quarter(0)
    x_send(3)

    def doc_backward(i, carry):
        hk = i // 2
        rows = pl.ds(pl.multiple_of(lax.rem(i, 2) * 256, 256), 256)
        lanes = pl.ds(pl.multiple_of(hk * HD, HD), HD)

        def get(cols):
            return edoc[hk, rows, cols], sdoc[hk, rows, cols]

        dk, dv = backward(k_ref[rows, lanes], v_ref[rows, lanes], hk, get)
        dk_ref[rows, lanes] = dk.astype(BF16)
        dv_ref[rows, lanes] = dv.astype(BF16)
        return carry

    lax.fori_loop(0, 4, doc_backward, 0)
    acc[...] = pair_sum(0)
    for r in (2, 1, 3):
        remote(xs.at[r - 1], xr.at[r - 1], xss.at[r - 1], xrs.at[r - 1], doc_id(zh, x + r, core)).wait_recv()
        acc[...] += xr[r - 1].astype(F32)
    for r in (2, 1, 3):
        zs[r - 1] = acc[:, lax.rem(zh + r, 4)].astype(BF16)
        send(zs.at[r - 1], zr.at[r - 1], zss.at[r - 1], zrs.at[r - 1], doc_id(zh + r, x, core))
    for hd in range(4):
        cols = slice((hd % 2) * TOK, (hd % 2 + 1) * TOK)
        dq_ref[:, hd * HD : (hd + 1) * HD] = (dqt[hd // 2, :, cols] * SCALE).T.astype(BF16)
    total = acc[:, zh]
    for r in (2, 1, 3):
        remote(zs.at[r - 1], zr.at[r - 1], zss.at[r - 1], zrs.at[r - 1], doc_id(zh + r, x, core)).wait_recv()
        total = total + zr[r - 1].astype(F32)
    pdk_ref[...] = total[0].astype(BF16)
    pdv_ref[...] = total[1].astype(BF16)
    for c in started:
        c.wait_send()


def on_device(queries, keys, values, prefix_keys, prefix_values, out_grad, out_weight, doc_lengths):
    sd = jax.ShapeDtypeStruct
    vm = pl.BlockSpec(memory_space=pltpu.VMEM)
    dma = pltpu.SemaphoreType.DMA
    return pl.pallas_call(
        kernel,
        out_shape=(
            sd((TOK, 512), BF16),
            sd((TOK, 256), BF16),
            sd((TOK, 256), BF16),
            sd((64, 256), BF16),
            sd((64, 256), BF16),
        ),
        in_specs=[pl.BlockSpec(memory_space=pltpu.SMEM)] + [vm] * 6 + [pl.BlockSpec(memory_space=pl.ANY)],
        out_specs=(vm,) * 5,
        scratch_shapes=[
            pltpu.VMEM((8, TOK, FEAT), BF16),
            pltpu.VMEM((512, 4608), BF16),
            pltpu.VMEM((4608, 512), BF16),
            pltpu.VMEM((4, 4, 2, 64, 256), BF16),
            pltpu.VMEM((4, 4, 2, 64, 256), BF16),
            pltpu.VMEM((2, 4, 4, HD, QW), BF16),
            pltpu.VMEM((2, 4, 4, HD, QW), BF16),
            pltpu.VMEM((2, TOK, QW), BF16),
            pltpu.VMEM((2, TOK, QW), BF16),
            pltpu.VMEM((2, HD, QW), BF16),
            pltpu.VMEM((2, QW, HD), BF16),
            pltpu.VMEM((2, HD, QW), BF16),
            pltpu.VMEM((2, QW, HD), BF16),
            pltpu.VMEM((2, HD, QW), F32),
            pltpu.VMEM((2, HD, QW), F32),
            pltpu.VMEM((2, 8, QW), F32),
            pltpu.VMEM((2, 1, QW), F32),
            pltpu.VMEM((TOK, 512), F32),
            pltpu.VMEM((4, 2, 2, 4, 64, 256), BF16),
            pltpu.VMEM((4, 2, 4, 64, 256), BF16),
            pltpu.VMEM((3, 2, 4, 64, 256), BF16),
            pltpu.VMEM((3, 2, 4, 64, 256), BF16),
            pltpu.VMEM((2, 4, 64, 256), F32),
            pltpu.VMEM((3, 2, 64, 256), BF16),
            pltpu.VMEM((3, 2, 64, 256), BF16),
            dma,
            dma((7, NC)),
            dma((7, NC)),
            dma((2, 3)),
            dma((2, 3)),
            dma((2, 3)),
            dma((2, 3)),
            dma((2, 4)),
            dma((2, 4)),
            dma((4,)),
            dma((4,)),
            dma((3,)),
            dma((3,)),
            dma((3,)),
            dma((3,)),
        ],
        compiler_params=pltpu.CompilerParams(
            collective_id=0, has_side_effects=True, vmem_limit_bytes=60 * 1024 * 1024
        ),
    )(doc_lengths, queries, keys, values, prefix_keys, prefix_values, out_grad, out_weight)


def solution(mesh):
    return jax.shard_map(
        on_device,
        mesh=mesh,
        in_specs=(P("docs", "heads"),) * 6 + (P("heads", None), P("docs", None)),
        out_specs=(P("docs", "heads"),) * 5,
        check_vma=False,
    )
```

time: 389 us -> 102 us (0.26)
  waiting for transfers between devices: 286 us -> 0 us
  Pallas kernels: 0 us -> 90.8 us
  matrix products: 58.8 us -> 0 us
  between operations: 14 us -> 0.64 us
  other arithmetic: 10.9 us -> 0 us
  local copies, waits for them, and re-layouts: 17.6 us -> 10.1 us
    reduce_scatter x2 -> x0, waiting for transfers between devices: 151 us -> none  [the longest x1 91.3 us: on_device(): lax.psum_scatter(jnp.einsum('kgtp,tkgd->pkd', part, qrows, preferred_elem...]
    all_gather x3 -> x0, waiting for transfers between devices: 133 us -> none  [the longest x1 48.6 us: on_device(): lax.all_gather(prefix_keys, 'docs', axis=0, tiled=True)]
    pallas_call x0 -> x1, Pallas kernels: none -> 90.8 us  [on_device(): pl.pallas_call(kernel, out_shape=(sd((TOK, 512), BF16), sd((TOK, 256), BF...]
    dot_general x13 -> x0, matrix products: 58.8 us -> none  [the longest x1 13.2 us: on_device(): jnp.einsum('tkgd,pkd->kgtp', dout, pvrows, preferred_element_type=fl)]
    convert_element_type x2 -> x0, other arithmetic: 9.75 us -> none  [the longest x1 8.47 us: on_device(): b_pre = p_pre.astype(jnp.bfloat16)]
    convert_element_type x2 -> x0, local copies, waits for them, and re-layouts: 4.54 us -> none  [the longest x1 2.27 us: on_device(): prefix_key_grad = lax.psum_scatter(jnp.einsum('kgtp,tkgd->pkd', part, qro...]
    unnamed x25 -> x6, local copies, waits for them, and re-layouts: 5.83 us -> 10.1 us
    reshape x4 -> x0, local copies, waits for them, and re-layouts: 4.24 us -> none  [the longest x1 1.81 us: on_device(): vrows = values.reshape(tok, kv_local, HEAD_DIM)]
  transfers between devices with their start and end apart: 5 -> 0, of which waited for: 5 -> 0; matrix products, arithmetic and copies ran while one was open for 15% -> 0% of each run, Pallas kernels for 0% -> 0%
where the time goes in v1:
time: 102 us
  Pallas kernels  90.8 us (89%)
  local copies, waits for them, and re-layouts  10.1 us (10%)
    pallas_call x1, Pallas kernels, on_device(): pl.pallas_call(kernel, out_shape=(sd((TOK, 512), BF16), sd((TOK, 256), BF...  90.8 us
    unnamed x6, local copies, waits for them, and re-layouts  10.1 us

profile of v1, /device:TPU:1, one launch (start us, length us, event | category | flops | bytes accessed | tf_op | source)
XLA Modules:
  0.0 101.6 jit_solution(8547933174538537828)
XLA Ops:
  0.6 2.2 %copy.13.og_ref = bf16[512,576]{1,0:T(8,128)(2,1)} copy(bf16[512,576]{0,1:T(8,128)(2,1)} %param.13) | data formatting | bytes 1179648 | tf_op args[5]
  2.8 90.8 %shard_map.119 = (bf16[512,512]{1,0:T(8,128)(2,1)}, bf16[512,256]{1,0:T(8,128)(2,1)}, bf16[512,256]{1,0:T(8,128)(2,1)}, bf16[64,256]{1,0:T(8,128)(2,1)}, bf16[64,256]{1,0:T(8,128)(2,1)}) custom-call(s32[1,3]{1,0:T(1,128)} %len_ref.1, bf16[512,512]{1,0:T(8,128)(2,1)} %q_ref.1, bf16[512,256]{1,0:T(8,128)(2,1)} %k_ref.1, bf16[512,256]{1,0:T(8,128)(2,1)} %v_ref.1, ...), custom_call_target="tpu_custom_call" | custom-call | tf_op jit(solution)/shard_map/pallas_call | solution.py:339
  93.6 1.9 %copy.19 = bf16[512,512]{1,0:T(8,128)(2,1)} copy(bf16[512,512]{1,0:T(8,128)(2,1)} %get-tuple-element.10) | data formatting | bytes 1048576
  95.5 1.7 %copy.20 = bf16[512,256]{1,0:T(8,128)(2,1)} copy(bf16[512,256]{1,0:T(8,128)(2,1)} %get-tuple-element.11) | data formatting | bytes 524288
  97.2 1.7 %copy.21 = bf16[512,256]{1,0:T(8,128)(2,1)} copy(bf16[512,256]{1,0:T(8,128)(2,1)} %get-tuple-element.12) | data formatting | bytes 524288
  98.8 1.4 %copy.22 = bf16[64,256]{1,0:T(8,128)(2,1)} copy(bf16[64,256]{1,0:T(8,128)(2,1)} %get-tuple-element.13) | data formatting | bytes 65536
  100.2 1.4 %copy.23 = bf16[64,256]{1,0:T(8,128)(2,1)} copy(bf16[64,256]{1,0:T(8,128)(2,1)} %get-tuple-element.14) | data formatting | bytes 65536

commit v2 on v0

v2 whole, which is shorter than its diff:
```python
import jax
import jax.numpy as jnp
from jax import lax
from jax.experimental import pallas as pl
from jax.experimental.pallas import tpu as pltpu
from jax.sharding import PartitionSpec as P

HD = 128
SOFTCAP = 50.0
SCALE = 1.0 / 12.0
LOG2E = 1.4426950408889634
F32 = jnp.float32
BF16 = jnp.bfloat16
MESH = pl.DeviceIdType.MESH

TOK = 512
FEAT = 576
WIN = 640
NC = 4
CH = TOK // NC
QW = 1024
PRE = 2048
QR = 512


def dot(a, b, dims=((1,), (0,))):
    return lax.dot_general(a, b, (dims, ((), ())), preferred_element_type=F32)


def kernel(
    len_ref, q_hbm, k_hbm, v_hbm, pk_hbm, pv_hbm, og_hbm, w_hbm,
    dq_hbm, dk_hbm, dv_hbm, pdk_hbm, pdv_hbm,
    qb, kd, vd, gbuf, wraw, kbuf, vbuf, ebuf, sbuf, edoc, sdoc, qt, qs, dot_t, dos, ot, lsum, drow, hgt,
    pb, pr, xs, xc, xr, tacc, zs, zr, odq, odk, odv, opk, opv,
    ls, gs, gr, kzs, kzr, kxs, kxr, kcs, kcr, ps, prs, xss, xrs, zss, zrs, osem,
):
    d = lax.axis_index("docs")
    h = lax.axis_index("heads")
    core = lax.rem(d, 2)
    x = lax.rem(d // 2, 4)
    zh = d // 8
    zl = h // 4
    y = lax.rem(h, 4)

    def doc_id(zz, xx, cc):
        return {"docs": (lax.rem(zz + 4, 4) * 4 + lax.rem(xx + 4, 4)) * 2 + cc}

    def head_id(zz, yy):
        return {"heads": zz * 4 + lax.rem(yy + 4, 4)}

    other = doc_id(zh, x, 1 - core)
    xdev = {1: doc_id(zh, x + 1, core), -1: doc_id(zh, x - 1, core)}
    zdev = {1: doc_id(zh + 1, x, core), 2: doc_id(zh + 2, x, core), 3: doc_id(zh + 3, x, core)}
    ydev = {1: head_id(zl, y + 1), -1: head_id(zl, y - 1)}
    pdev = head_id(1 - zl, y)

    barrier = pltpu.get_barrier_semaphore()
    peers = (other, xdev[1], xdev[-1], zdev[1], zdev[2], zdev[3], ydev[1], ydev[-1], pdev)
    for p in peers:
        pl.semaphore_signal(barrier, inc=1, device_id=p, device_id_type=MESH)

    def slot_of(ry, rl):
        return (ry % 4) * 2 + rl

    def pad_of(ry):
        return lax.rem(y + ry % 4, 2)

    def rows_of(ry):
        return pl.ds(pl.multiple_of(pad_of(ry) * (WIN - FEAT), WIN - FEAT), FEAT)

    local = [
        pltpu.make_async_copy(q_hbm, qb, ls.at[0]),
        pltpu.make_async_copy(k_hbm, kd, ls.at[1]),
        pltpu.make_async_copy(v_hbm, vd, ls.at[2]),
        pltpu.make_async_copy(pk_hbm, kbuf.at[0:64], ls.at[3]),
        pltpu.make_async_copy(pv_hbm, vbuf.at[0:64], ls.at[4]),
        pltpu.make_async_copy(og_hbm, gbuf.at[0, rows_of(0)], ls.at[5]),
        pltpu.make_async_copy(w_hbm, wraw, ls.at[6]),
    ]
    for c in local:
        c.start()
    pl.semaphore_wait(barrier, len(peers))

    started = []

    def remote(src, dst, ssem, rsem, device):
        return pltpu.make_async_remote_copy(
            src_ref=src, dst_ref=dst, send_sem=ssem, recv_sem=rsem, device_id=device, device_id_type=MESH
        )

    def send(*args):
        c = remote(*args)
        c.start()
        started.append(c)

    def landed(dst, ssem, rsem):
        remote(dst, dst, ssem, rsem, other).wait_recv()

    def g_route(kind, c):
        s = 1 if c % 2 == 0 else -1
        return [
            ((0, 0), ydev[s], (-s, 0)),
            ((0, 0), ydev[-s], (s, 0)),
            ((0, 0), pdev, (0, 1)),
            ((0, 1), ydev[s], (-s, 1)),
            ((s, 0), ydev[-s], (2, 0)),
            ((s, 0), pdev, (s, 1)),
            ((-s, 1), ydev[s], (2, 1)),
        ][kind]

    def g_at(where, c):
        return gbuf.at[slot_of(*where), rows_of(where[0]), pl.ds(c * CH, CH)]

    def g_send(kind, c):
        here, to, there = g_route(kind, c)
        at = gbuf.at[slot_of(*there), rows_of(here[0]), pl.ds(c * CH, CH)]
        src = og_hbm.at[:, pl.ds(c * CH, CH)] if kind < 3 else g_at(here, c)
        send(src, at, gs.at[kind, c], gr.at[kind, c], to)

    def g_wait(kind, c):
        landed(g_at(g_route(kind, c)[2], c), gs.at[kind, c], gr.at[kind, c])

    pre = ((0, kbuf, pk_hbm), (1, vbuf, pv_hbm))

    def z_rows(rz):
        return pl.ds(rz * 64, 64)

    def x_rows(rx, piece):
        return pl.ds(rx * QR + (0 if piece == 0 else 64), 64 if piece == 0 else 192)

    def c_rows(rx, rc):
        return pl.ds(rx * QR + rc * 256, 256)

    for i, buf, src in pre:
        send(src, buf.at[z_rows(3)], kzs.at[i, 0], kzr.at[i, 0], zdev[1])
        send(src, buf.at[z_rows(1)], kzs.at[i, 1], kzr.at[i, 1], zdev[3])
    for i, buf, src in pre:
        send(src, buf.at[x_rows(3, 0)], kxs.at[i, 0, 0], kxr.at[i, 0, 0], xdev[1])
        send(src, buf.at[x_rows(1, 0)], kxs.at[i, 0, 1], kxr.at[i, 0, 1], xdev[-1])
    for c in range(NC):
        g_send(0, c)
        g_send(1, c)
    g_send(2, 0)

    for ry in range(4):
        zero = pl.ds(pl.multiple_of((1 - pad_of(ry)) * FEAT, WIN - FEAT), WIN - FEAT)
        for rl in range(2):
            gbuf[slot_of(ry, rl), zero, :] = jnp.zeros((WIN - FEAT, TOK), BF16)
    for c in local[:3]:
        c.wait()
    for hd in range(4):
        blk = qb[:, hd * HD : (hd + 1) * HD]
        qs[hd // 2, (hd % 2) * TOK : (hd % 2 + 1) * TOK, :] = blk
        qt[hd // 2, :, (hd % 2) * TOK : (hd % 2 + 1) * TOK] = blk.T

    b0 = len_ref[0, 0]
    b1 = b0 + len_ref[0, 1]
    b2 = b1 + len_ref[0, 2]

    def segment(p):
        return (p >= b0).astype(jnp.int32) + (p >= b1).astype(jnp.int32) + (p >= b2).astype(jnp.int32)

    def weights(kk, hk, cols, mask):
        t = jnp.tanh(dot(kk, qt[hk, :, cols]) * (SCALE / SOFTCAP))
        e = jnp.exp2(t * (SOFTCAP * LOG2E))
        if mask is not None:
            e = jnp.where(mask, e, 0.0)
        return e, e * (1.0 - t * t)

    def partial_sums(e):
        return jnp.sum(e.reshape(e.shape[0] // 8, 8, e.shape[1]), axis=0)

    def doc_forward(hk):
        lsum[hk] = jnp.zeros((8, QW), F32)
        for j in range(4):
            rows = slice(j * HD, (j + 1) * HD)
            lo, hi = j * HD, min(TOK, (j + 3) * HD)
            key = lo + lax.broadcasted_iota(jnp.int32, (HD, hi - lo), 0)
            row = lo + lax.broadcasted_iota(jnp.int32, (HD, hi - lo), 1)
            mask = (key <= row) & (segment(key) == segment(row))
            for g in range(2):
                cols = slice(g * TOK + lo, g * TOK + hi)
                e, s = weights(kd[rows, hk * HD : (hk + 1) * HD], hk, cols, mask)
                lsum[hk, :, cols] += partial_sums(e)
                edoc[hk, rows, cols] = e.astype(BF16)
                sdoc[hk, rows, cols] = s.astype(BF16)
                for a, b in ((0, lo), (hi, TOK)):
                    if a < b:
                        edoc[hk, rows, g * TOK + a : g * TOK + b] = jnp.zeros((HD, b - a), BF16)
                        sdoc[hk, rows, g * TOK + a : g * TOK + b] = jnp.zeros((HD, b - a), BF16)

    def pre_forward(rx):
        def one(hk, carry):
            rows = slice(rx * QR, (rx + 1) * QR)
            lanes = pl.ds(pl.multiple_of(hk * HD, HD), HD)
            e, s = weights(kbuf[rows, lanes], hk, slice(None), None)
            lsum[hk] += partial_sums(e)
            ebuf[hk, rows, :] = e.astype(BF16)
            sbuf[hk, rows, :] = s.astype(BF16)
            return carry

        lax.fori_loop(0, 2, one, 0)

    def x_pass(piece):
        for i, buf, _ in pre:
            got, to = ((3, 1), (1, -1))[i]
            side = 0 if got == 3 else 1
            landed(buf.at[x_rows(got, piece)], kxs.at[i, piece, side], kxr.at[i, piece, side])
            send(buf.at[x_rows(got, piece)], buf.at[x_rows(2, piece)], kxs.at[i, piece, 2], kxr.at[i, piece, 2], xdev[to])

    def x_rest(piece):
        for i, buf, _ in pre:
            got = (1, 3)[i]
            side = 0 if got == 3 else 1
            landed(buf.at[x_rows(got, piece)], kxs.at[i, piece, side], kxr.at[i, piece, side])

    def x_across(piece):
        for i, buf, _ in pre:
            landed(buf.at[x_rows(2, piece)], kxs.at[i, piece, 2], kxr.at[i, piece, 2])

    def core_send(rx):
        for i, buf, _ in pre:
            send(buf.at[c_rows(rx, 0)], buf.at[c_rows(rx, 1)], kcs.at[i, rx], kcr.at[i, rx], other)

    def core_wait(rx):
        for i, buf, _ in pre:
            landed(buf.at[c_rows(rx, 1)], kcs.at[i, rx], kcr.at[i, rx])

    def g_forward(c):
        g_wait(2, c)
        g_send(3, c)
        g_wait(1, c)
        g_send(4, c)
        g_send(5, c)

    def g_last(c):
        g_wait(3, c)
        g_send(6, c)

    doc_forward(0)

    landed(kbuf.at[z_rows(3)], kzs.at[0, 0], kzr.at[0, 0])
    send(kbuf.at[z_rows(3)], kbuf.at[z_rows(2)], kzs.at[0, 2], kzr.at[0, 2], zdev[1])
    landed(vbuf.at[z_rows(1)], kzs.at[1, 1], kzr.at[1, 1])
    send(vbuf.at[z_rows(1)], vbuf.at[z_rows(2)], kzs.at[1, 2], kzr.at[1, 2], zdev[3])
    landed(kbuf.at[z_rows(1)], kzs.at[0, 1], kzr.at[0, 1])
    landed(vbuf.at[z_rows(3)], kzs.at[1, 0], kzr.at[1, 0])
    for c in range(1, NC):
        g_send(2, c)
    x_pass(0)
    doc_forward(1)
    for i, buf, _ in pre:
        landed(buf.at[z_rows(2)], kzs.at[i, 2], kzr.at[i, 2])
        send(buf.at[x_rows(0, 1)], buf.at[x_rows(3, 1)], kxs.at[i, 1, 0], kxr.at[i, 1, 0], xdev[1])
        send(buf.at[x_rows(0, 1)], buf.at[x_rows(1, 1)], kxs.at[i, 1, 1], kxr.at[i, 1, 1], xdev[-1])
    for c in local[3:5]:
        c.wait()
    core_send(0)
    g_forward(0)
    core_wait(0)
    pre_forward(0)
    g_forward(1)
    x_pass(1)
    x_rest(0)
    x_rest(1)
    core_send(3)
    core_send(1)
    g_forward(2)
    g_last(0)
    core_wait(3)
    pre_forward(3)
    x_across(0)
    x_across(1)
    core_send(2)
    g_forward(3)
    core_wait(1)
    pre_forward(1)
    g_last(1)
    core_wait(2)
    pre_forward(2)
    g_last(2)

    for hk in range(2):
        lanes = slice(hk * HD, (hk + 1) * HD)
        ot[hk] = dot(vbuf[:, lanes], ebuf[hk], ((0,), (0,))) + dot(vd[:, lanes], edoc[hk], ((0,), (0,)))

    def w_window(ry, rl):
        yy = lax.rem(y + ry % 4, 4)
        src = (zl + rl - 2 * zl * rl) * 4 + yy
        first = (src // 2) * 9 + 4 * lax.rem(src, 2)
        return wraw[:, pl.ds(pl.multiple_of(first * HD, HD), WIN)]

    def project(where, even, odd, waited):
        for c in range(NC):
            if not waited[c % 2]:
                g_wait(odd if c % 2 else even, c)
        hgt[...] += dot(w_window(*where), gbuf[slot_of(*where)])

    for c in local[5:]:
        c.wait()
    hgt[...] = dot(w_window(0, 0), gbuf[0])
    project((1, 0), 1, 0, (True, False))
    project((3, 0), 0, 1, (False, True))
    project((0, 1), 2, 2, (True, True))
    g_last(3)
    project((2, 0), 4, 4, (False, False))
    project((1, 1), 5, 3, (False, True))
    project((3, 1), 3, 5, (True, False))
    project((2, 1), 6, 6, (False, False))

    for hd in range(4):
        hk, cols = hd // 2, slice((hd % 2) * TOK, (hd % 2 + 1) * TOK)
        g = hgt[hd * HD : (hd + 1) * HD, :].astype(BF16).astype(F32)
        inv = 1.0 / jnp.sum(lsum[hk, :, cols], axis=0, keepdims=True)
        scaled = (g * inv).astype(BF16)
        drow[hk, :, cols] = jnp.sum(g * ot[hk, :, cols], axis=0, keepdims=True) * (inv * inv)
        dot_t[hk, :, cols] = scaled
        dos[hk, cols, :] = scaled.T

    def dv_quarter(rx):
        for hk in range(2):
            dv = dot(ebuf[hk, rx * QR : (rx + 1) * QR, :], dos[hk])
            pb[0, rx, :, :, hk * HD : (hk + 1) * HD] = dv.astype(BF16).reshape(2, 256, HD)

    def logit_grads(vv, hk, buf, rows):
        for n in range(2):
            cols = slice(n * TOK, (n + 1) * TOK)
            dp = dot(vv, dot_t[hk, :, cols]) - drow[hk, :, cols]
            buf[hk, rows, cols] = (buf[hk, rows, cols].astype(F32) * dp).astype(BF16)

    def dk_quarter(rx):
        rows = slice(rx * QR, (rx + 1) * QR)
        for hk in range(2):
            lanes = slice(hk * HD, (hk + 1) * HD)
            logit_grads(vbuf[rows, lanes], hk, sbuf, rows)
            dk = dot(sbuf[hk, rows, :], qs[hk]) * SCALE
            pb[1, rx, :, :, lanes] = dk.astype(BF16).reshape(2, 256, HD)

    def pair_send(a, rx):
        send(pb.at[a, rx, 1], pr.at[a, rx], ps.at[a, rx], prs.at[a, rx], other)

    def pair_sum(a, rx):
        landed(pr.at[a, rx], ps.at[a, rx], prs.at[a, rx])
        return pb[a, rx, 0].astype(F32) + pr[a, rx].astype(F32)

    def x_far(a):
        xs[a, 2] = pair_sum(a, 2).astype(BF16)
        send(xs.at[a, 2, 0:128], xc.at[a, 0], xss.at[a, 0], xrs.at[a, 0], xdev[1])
        send(xs.at[a, 2, 128:256], xc.at[a, 1], xss.at[a, 1], xrs.at[a, 1], xdev[-1])

    def x_near(a, n):
        s = pair_sum(a, 1 + 2 * n)
        landed(xc.at[a, n], xss.at[a, n], xrs.at[a, n])
        half = slice(n * 128, (n + 1) * 128)
        rest = slice((1 - n) * 128, (2 - n) * 128)
        xs[a, n, half] = (s[half] + xc[a, n].astype(F32)).astype(BF16)
        xs[a, n, rest] = s[rest].astype(BF16)
        send(xs.at[a, n], xr.at[a, n], xss.at[a, 2 + n], xrs.at[a, 2 + n], xdev[1 - 2 * n])

    def x_total(a):
        t = pair_sum(a, 0)
        for n in range(2):
            landed(xr.at[a, n], xss.at[a, 2 + n], xrs.at[a, 2 + n])
            t = t + xr[a, n].astype(F32)
        tacc[a] = t[0:64]
        zs[a] = t[64:256].astype(BF16)
        for rz in (2, 1, 3):
            piece = slice((rz - 1) * 64, rz * 64)
            send(zs.at[a, piece], zr.at[a, rz - 1], zss.at[a, rz - 1], zrs.at[a, rz - 1], zdev[rz])

    outs = []

    def put(src, dst, n):
        c = pltpu.make_async_copy(src, dst, osem.at[n])
        c.start()
        outs.append(c)

    def z_total(a):
        t = tacc[a]
        for n in range(3):
            landed(zr.at[a, n], zss.at[a, n], zrs.at[a, n])
            t = t + zr[a, n].astype(F32)
        out, dst = ((opv, pdv_hbm), (opk, pdk_hbm))[a]
        out[...] = t.astype(BF16)
        put(out, dst, a)

    dv_quarter(2)
    pair_send(0, 2)
    dv_quarter(1)
    pair_send(0, 1)
    x_far(0)
    dv_quarter(3)
    pair_send(0, 3)
    dv_quarter(0)
    pair_send(0, 0)
    dk_quarter(2)
    pair_send(1, 2)
    x_near(0, 0)
    x_near(0, 1)
    dk_quarter(1)
    pair_send(1, 1)
    x_far(1)
    dk_quarter(3)
    pair_send(1, 3)
    dk_quarter(0)
    pair_send(1, 0)
    x_near(1, 0)
    x_near(1, 1)
    x_total(0)
    for hk in range(2):
        lanes = slice(hk * HD, (hk + 1) * HD)
        logit_grads(vd[:, lanes], hk, sdoc, slice(None))
        odk[:, lanes] = (dot(sdoc[hk], qs[hk]) * SCALE).astype(BF16)
        odv[:, lanes] = dot(edoc[hk], dos[hk]).astype(BF16)
    put(odk, dk_hbm, 2)
    put(odv, dv_hbm, 3)
    x_total(1)

    for hk in range(2):
        lanes = slice(hk * HD, (hk + 1) * HD)
        t = dot(kbuf[:, lanes], sbuf[hk], ((0,), (0,))) + dot(kd[:, lanes], sdoc[hk], ((0,), (0,)))
        for g in range(2):
            hd = hk * 2 + g
            odq[:, hd * HD : (hd + 1) * HD] = (t[:, g * TOK : (g + 1) * TOK] * SCALE).astype(BF16).T
    put(odq, dq_hbm, 4)
    z_total(0)
    z_total(1)
    for c in started:
        c.wait_send()
    for c in outs:
        c.wait()


def finish(*refs):
    for a, b in zip(refs[:5], refs[5:]):
        b[...] = a[...]


def on_device(queries, keys, values, prefix_keys, prefix_values, out_grad, out_weight, doc_lengths):
    sd = jax.ShapeDtypeStruct
    hbm = pl.BlockSpec(memory_space=pl.ANY)
    vm = pltpu.VMEM
    dma = pltpu.SemaphoreType.DMA
    shapes = (
        sd((TOK, 512), BF16),
        sd((TOK, 256), BF16),
        sd((TOK, 256), BF16),
        sd((64, 256), BF16),
        sd((64, 256), BF16),
    )
    grads = pl.pallas_call(
        kernel,
        out_shape=shapes,
        in_specs=[pl.BlockSpec(memory_space=pltpu.SMEM)] + [hbm] * 7,
        out_specs=(hbm,) * 5,
        scratch_shapes=[
            vm((TOK, 512), BF16),
            vm((TOK, 256), BF16),
            vm((TOK, 256), BF16),
            vm((8, WIN, TOK), BF16),
            vm((512, 4608), BF16),
            vm((PRE, 256), BF16),
            vm((PRE, 256), BF16),
            vm((2, PRE, QW), BF16),
            vm((2, PRE, QW), BF16),
            vm((2, TOK, QW), BF16),
            vm((2, TOK, QW), BF16),
            vm((2, HD, QW), BF16),
            vm((2, QW, HD), BF16),
            vm((2, HD, QW), BF16),
            vm((2, QW, HD), BF16),
            vm((2, HD, QW), F32),
            vm((2, 8, QW), F32),
            vm((2, 1, QW), F32),
            vm((512, TOK), F32),
            vm((2, 4, 2, 256, 256), BF16),
            vm((2, 4, 256, 256), BF16),
            vm((2, 3, 256, 256), BF16),
            vm((2, 2, 128, 256), BF16),
            vm((2, 2, 256, 256), BF16),
            vm((2, 64, 256), F32),
            vm((2, 192, 256), BF16),
            vm((2, 3, 64, 256), BF16),
            vm((TOK, 512), BF16),
            vm((TOK, 256), BF16),
            vm((TOK, 256), BF16),
            vm((64, 256), BF16),
            vm((64, 256), BF16),
            dma((7,)),
            dma((7, NC)),
            dma((7, NC)),
            dma((2, 3)),
            dma((2, 3)),
            dma((2, 2, 3)),
            dma((2, 2, 3)),
            dma((2, 4)),
            dma((2, 4)),
            dma((2, 4)),
            dma((2, 4)),
            dma((2, 4)),
            dma((2, 4)),
            dma((2, 3)),
            dma((2, 3)),
            dma((5,)),
        ],
        compiler_params=pltpu.CompilerParams(
            collective_id=0, has_side_effects=True, vmem_limit_bytes=60 * 1024 * 1024
        ),
    )(doc_lengths, queries, keys, values, prefix_keys, prefix_values, out_grad.T, out_weight)
    return pl.pallas_call(
        finish,
        out_shape=shapes,
        in_specs=[pl.BlockSpec(memory_space=vm)] * 5,
        out_specs=(pl.BlockSpec(memory_space=vm),) * 5,
    )(*grads)


def solution(mesh):
    return jax.shard_map(
        on_device,
        mesh=mesh,
        in_specs=(P("docs", "heads"),) * 6 + (P("heads", None), P("docs", None)),
        out_specs=(P("docs", "heads"),) * 5,
        check_vma=False,
    )
```

time: 389 us -> 69.8 us (0.18)
  waiting for transfers between devices: 286 us -> 0 us
  Pallas kernels: 0 us -> 68.4 us
  matrix products: 58.8 us -> 0 us
  local copies, waits for them, and re-layouts: 17.6 us -> 0 us
  between operations: 14 us -> 0.64 us
  other arithmetic: 10.9 us -> 0 us
    reduce_scatter x2 -> x0, waiting for transfers between devices: 151 us -> none  [the longest x1 91.3 us: on_device(): lax.psum_scatter(jnp.einsum('kgtp,tkgd->pkd', part, qrows, preferred_elem...]
    all_gather x3 -> x0, waiting for transfers between devices: 133 us -> none  [the longest x1 48.6 us: on_device(): lax.all_gather(prefix_keys, 'docs', axis=0, tiled=True)]
    pallas_call x0 -> x2, Pallas kernels: none -> 68.4 us  [the longest x1 66.2 us: on_device(): pl.pallas_call(kernel, out_shape=shapes, in_specs=[pl.BlockSpec(memory_sp...]
    dot_general x13 -> x0, matrix products: 58.8 us -> none  [the longest x1 13.2 us: on_device(): jnp.einsum('tkgd,pkd->kgtp', dout, pvrows, preferred_element_type=fl)]
    convert_element_type x2 -> x0, other arithmetic: 9.75 us -> none  [the longest x1 8.47 us: on_device(): b_pre = p_pre.astype(jnp.bfloat16)]
    unnamed x25 -> x0, local copies, waits for them, and re-layouts: 5.83 us -> none
    convert_element_type x2 -> x0, local copies, waits for them, and re-layouts: 4.54 us -> none  [the longest x1 2.27 us: on_device(): prefix_key_grad = lax.psum_scatter(jnp.einsum('kgtp,tkgd->pkd', part, qro...]
    reshape x4 -> x0, local copies, waits for them, and re-layouts: 4.24 us -> none  [the longest x1 1.81 us: on_device(): vrows = values.reshape(tok, kv_local, HEAD_DIM)]
  transfers between devices with their start and end apart: 5 -> 0, of which waited for: 5 -> 0; matrix products, arithmetic and copies ran while one was open for 15% -> 0% of each run, Pallas kernels for 0% -> 0%
where the time goes in v2:
time: 69.8 us; the launch traced here: 69.1 us
  Pallas kernels  68.4 us (98%)
    pallas_call x1, Pallas kernels, on_device(): pl.pallas_call(kernel, out_shape=shapes, in_specs=[pl.BlockSpec(memory_sp...  66.2 us
    pallas_call x1, Pallas kernels, on_device(): pl.pallas_call(finish, out_shape=shapes, in_specs=[pl.BlockSpec(memory_sp...  2.2 us

profile of v2, /device:TPU:1, one launch (start us, length us, event | category | flops | bytes accessed | tf_op | source)
XLA Modules:
  0.0 69.1 jit_solution(16813236807965276474)
XLA Ops:
  0.6 66.2 %shard_map.119 = (bf16[512,512]{1,0:T(8,128)(2,1)}, bf16[512,256]{1,0:T(8,128)(2,1)}, bf16[512,256]{1,0:T(8,128)(2,1)}, bf16[64,256]{1,0:T(8,128)(2,1)}, bf16[64,256]{1,0:T(8,128)(2,1)}) custom-call(s32[1,3]{1,0:T(1,128)} %len_ref.1, bf16[512,512]{1,0:T(8,128)(2,1)} %q_hbm.1, bf16[512,256]{1,0:T(8,128)(2,1)} %k_hbm.1, bf16[512,256]{1,0:T(8,128)(2,1)} %v_hbm.1, ...), custom_call_target="tpu_custom_call" | custom-call | tf_op jit(solution)/shard_map/pallas_call | solution.py:451
  66.9 2.2 %shard_map.120 = (bf16[512,512]{1,0:T(8,128)(2,1)}, bf16[512,256]{1,0:T(8,128)(2,1)}, bf16[512,256]{1,0:T(8,128)(2,1)}, bf16[64,256]{1,0:T(8,128)(2,1)}, bf16[64,256]{1,0:T(8,128)(2,1)}) custom-call(bf16[512,512]{1,0:T(8,128)(2,1)} %get-tuple-element.10.refs_0_, bf16[512,256]{1,0:T(8,128)(2,1)} %get-tuple-element.11.refs_1_, ...), custom_call_target="tpu_custom_call" | custom-call | tf_op jit(solution)/shard_map/pallas_call | solution.py:510

commit v3 on v2

v3 whole, which is shorter than its diff:
```python
import jax
import jax.numpy as jnp
from jax import lax
from jax.experimental import pallas as pl
from jax.experimental.pallas import tpu as pltpu
from jax.sharding import PartitionSpec as P

HD = 128
SOFTCAP = 50.0
SCALE = 1.0 / 12.0
LOG2E = 1.4426950408889634
F32 = jnp.float32
BF16 = jnp.bfloat16
MESH = pl.DeviceIdType.MESH

TOK = 512
FEAT = 576
LAY = 4 * FEAT
NC = 4
CH = TOK // NC
QW = 1024
PRE = 2048
QR = 512


def dot(a, b, dims=((1,), (0,))):
    return lax.dot_general(a, b, (dims, ((), ())), preferred_element_type=F32)


def kernel(
    len_ref, q_hbm, k_hbm, v_hbm, pk_hbm, pv_hbm, og_hbm, w_hbm,
    dq_hbm, dk_hbm, dv_hbm, pdk_hbm, pdv_hbm,
    qb, kd, vd, gl, wl, wp, hs, hr, kbuf, vbuf, ebuf, sbuf, edoc, sdoc, qt, qs, dot_t, dos, ot, lsum, drow, hgt,
    pb, pr, xs, xr, tacc, zs, zr, odq, odk, odv, opk, opv,
    ls, gs, gr, hss, hrs, wzs, wzr, wxs, wxr, wcs, wcr, kzs, kzr, kxs, kxr, kcs, kcr, ps, prs, xss, xrs, zss, zrs, osem,
):
    d = lax.axis_index("docs")
    h = lax.axis_index("heads")
    core = lax.rem(d, 2)
    x = lax.rem(d // 2, 4)
    zh = d // 8
    zl = h // 4
    y = lax.rem(h, 4)

    def doc_id(zz, xx, cc):
        return {"docs": (lax.rem(zz + 4, 4) * 4 + lax.rem(xx + 4, 4)) * 2 + cc}

    def head_id(zz, yy):
        return {"heads": zz * 4 + lax.rem(yy + 4, 4)}

    other = doc_id(zh, x, 1 - core)
    xdev = {1: doc_id(zh, x + 1, core), -1: doc_id(zh, x - 1, core), -2: doc_id(zh, x - 2, core)}
    xdev[-3] = xdev[1]
    zdev = {1: doc_id(zh + 1, x, core), 2: doc_id(zh + 2, x, core), 3: doc_id(zh + 3, x, core)}
    ydev = {1: head_id(zl, y + 1), -1: head_id(zl, y - 1)}
    pdev = head_id(1 - zl, y)
    zz = lax.rem(zh + 2 * zl + 3, 4)
    wdev = {"docs": (zz * 4 + x) * 2 + core, "heads": (1 - zl) * 4 + y}

    barrier = pltpu.get_barrier_semaphore()
    peers = (other, xdev[1], xdev[-1], xdev[-2], zdev[1], zdev[2], zdev[3], ydev[1], ydev[-1], pdev, wdev)
    for p in peers:
        pl.semaphore_signal(barrier, inc=1, device_id=p, device_id_type=MESH)

    def g_rows(ry):
        return pl.ds(pl.multiple_of(lax.rem(y + ry + 4, 4) * FEAT, FEAT), FEAT)

    def layer(zz):
        return pl.ds(pl.multiple_of(zz * LAY, LAY), LAY)

    local = [
        pltpu.make_async_copy(q_hbm, qb, ls.at[0]),
        pltpu.make_async_copy(k_hbm, kd, ls.at[1]),
        pltpu.make_async_copy(v_hbm, vd, ls.at[2]),
        pltpu.make_async_copy(pk_hbm, kbuf.at[0, 0, 0], ls.at[3]),
        pltpu.make_async_copy(pv_hbm, vbuf.at[0, 0, 0], ls.at[4]),
        pltpu.make_async_copy(og_hbm, gl.at[g_rows(0)], ls.at[5]),
        pltpu.make_async_copy(w_hbm.at[:, layer(zl)], wl, ls.at[6]),
    ]
    for c in local:
        c.start()
    pl.semaphore_wait(barrier, len(peers))

    started = []

    def remote(src, dst, ssem, rsem, device):
        return pltpu.make_async_remote_copy(
            src_ref=src, dst_ref=dst, send_sem=ssem, recv_sem=rsem, device_id=device, device_id_type=MESH
        )

    def send(*args):
        c = remote(*args)
        c.start()
        started.append(c)

    def landed(dst, ssem, rsem):
        remote(dst, dst, ssem, rsem, other).wait_recv()

    def g_route(kind, c):
        s = 1 if c % 2 == 0 else -1
        return ((0, ydev[s], -s), (0, ydev[-s], s), (s, ydev[-s], 2))[kind]

    def g_send(kind, c):
        ry, to, _ = g_route(kind, c)
        cols = pl.ds(c * CH, CH)
        at = gl.at[g_rows(ry), cols]
        send(og_hbm.at[:, cols] if kind < 2 else at, at, gs.at[kind, c], gr.at[kind, c], to)

    def g_wait(kind, c):
        landed(gl.at[g_rows(g_route(kind, c)[2]), pl.ds(c * CH, CH)], gs.at[kind, c], gr.at[kind, c])

    def g_forward(c):
        g_wait(1, c)
        g_send(2, c)

    def w_rows(odd, rc, part):
        first = lax.rem(x + odd, 2) * 256 + (core if rc == 0 else 1 - core) * 128
        if part is None:
            return pl.ds(pl.multiple_of(first, 128), 128)
        return pl.ds(pl.multiple_of(first + part * 64, 64), 64)

    def w_send():
        for part, to in ((0, pdev), (1, wdev)):
            rows = w_rows(0, 0, part)
            send(w_hbm.at[rows, layer(1 - zl)], wp.at[rows], wzs.at[part], wzr.at[part], to)

    def w_spread(part):
        rows = w_rows(0, 0, part)
        landed(wp.at[rows], wzs.at[part], wzr.at[part])
        send(wp.at[rows], wp.at[rows], wxs.at[part], wxr.at[part], xdev[1 - 2 * part])

    def w_core(odd):
        rows = w_rows(odd, 0, None)
        send(wp.at[rows], wp.at[rows], wcs.at[odd], wcr.at[odd], other)

    def w_across():
        for part in range(2):
            landed(wp.at[w_rows(1, 0, part)], wxs.at[part], wxr.at[part])
        w_core(1)

    def w_wait(odd):
        landed(wp.at[w_rows(odd, 1, None)], wcs.at[odd], wcr.at[odd])

    pre = ((0, kbuf, pk_hbm), (1, vbuf, pv_hbm))
    for i, buf, src in pre:
        send(src, buf.at[0, 0, 3], kzs.at[i, 2], kzr.at[i, 2], zdev[1])
        send(src, buf.at[0, 0, 1], kzs.at[i, 0], kzr.at[i, 0], zdev[3])
    w_send()
    for i, buf, src in pre:
        send(src, buf.at[0, 0, 2], kzs.at[i, 1], kzr.at[i, 1], zdev[2])
    for i, buf, src in pre:
        for rx in (1, 3, 2):
            send(src, buf.at[rx, 0, 0], kxs.at[i, 0, rx - 1], kxr.at[i, 0, rx - 1], xdev[-rx])
    for c in range(NC):
        g_send(0, c)
        g_send(1, c)
    for c in local[:3]:
        c.wait()
    for hd in range(4):
        blk = qb[:, hd * HD : (hd + 1) * HD]
        qs[hd // 2, (hd % 2) * TOK : (hd % 2 + 1) * TOK, :] = blk
        qt[hd // 2, :, (hd % 2) * TOK : (hd % 2 + 1) * TOK] = blk.T

    b0 = len_ref[0, 0]
    b1 = b0 + len_ref[0, 1]
    b2 = b1 + len_ref[0, 2]

    def segment(p):
        return (p >= b0).astype(jnp.int32) + (p >= b1).astype(jnp.int32) + (p >= b2).astype(jnp.int32)

    def weights(kk, hk, cols, mask):
        t = jnp.tanh(dot(kk, qt[hk, :, cols]) * (SCALE / SOFTCAP))
        e = jnp.exp2(t * (SOFTCAP * LOG2E))
        if mask is not None:
            e = jnp.where(mask, e, 0.0)
        return e, e * (1.0 - t * t)

    def partial_sums(e):
        return jnp.sum(e.reshape(e.shape[0] // 8, 8, e.shape[1]), axis=0)

    def doc_forward(hk):
        lsum[hk] = jnp.zeros((8, QW), F32)
        for j in range(4):
            rows = slice(j * HD, (j + 1) * HD)
            lo, hi = j * HD, min(TOK, (j + 3) * HD)
            key = lo + lax.broadcasted_iota(jnp.int32, (HD, hi - lo), 0)
            row = lo + lax.broadcasted_iota(jnp.int32, (HD, hi - lo), 1)
            mask = (key <= row) & (segment(key) == segment(row))
            for g in range(2):
                cols = slice(g * TOK + lo, g * TOK + hi)
                e, s = weights(kd[rows, hk * HD : (hk + 1) * HD], hk, cols, mask)
                lsum[hk, :, cols] += partial_sums(e)
                edoc[hk, rows, cols] = e.astype(BF16)
                sdoc[hk, rows, cols] = s.astype(BF16)
                for a, b in ((0, lo), (hi, TOK)):
                    if a < b:
                        edoc[hk, rows, g * TOK + a : g * TOK + b] = jnp.zeros((HD, b - a), BF16)
                        sdoc[hk, rows, g * TOK + a : g * TOK + b] = jnp.zeros((HD, b - a), BF16)

    def pre_forward(rz):
        def one(hk, carry):
            lanes = pl.ds(pl.multiple_of(hk * HD, HD), HD)
            e, s = weights(kbuf[:, :, rz, :, lanes].reshape(QR, HD), hk, slice(None), None)
            lsum[hk] += partial_sums(e)
            ebuf[hk, :, :, rz] = e.astype(BF16).reshape(4, 2, 64, QW)
            sbuf[hk, :, :, rz] = s.astype(BF16).reshape(4, 2, 64, QW)
            return carry

        lax.fori_loop(0, 2, one, 0)

    def z_landed(rz):
        for i, buf, _ in pre:
            landed(buf.at[0, 0, rz], kzs.at[i, rz - 1], kzr.at[i, rz - 1])

    def x_near(rz):
        for i, buf, _ in pre:
            for rx in (1, 3):
                send(buf.at[0, 0, rz], buf.at[rx, 0, rz], kxs.at[i, rz, rx - 1], kxr.at[i, rz, rx - 1], xdev[-rx])

    def x_landed(i, rx, rz):
        landed(pre[i][1].at[rx, 0, rz], kxs.at[i, rz, rx - 1], kxr.at[i, rz, rx - 1])

    def x_pass(rz):
        for i, got, to in ((0, 3, 1), (1, 1, -1)):
            x_landed(i, got, rz)
            buf = pre[i][1]
            send(buf.at[got, 0, rz], buf.at[2, 0, rz], kxs.at[i, rz, 1], kxr.at[i, rz, 1], xdev[to])

    def core_send(rz):
        for i, buf, _ in pre:
            for rx in (1, 3, 2):
                if rz == 0 or rx == 2 or rx == (1, 3)[i]:
                    x_landed(i, rx, rz)
            send(buf.at[:, 0, rz], buf.at[:, 1, rz], kcs.at[i, rz], kcr.at[i, rz], other)

    def core_wait(rz):
        for i, buf, _ in pre:
            landed(buf.at[:, 1, rz], kcs.at[i, rz], kcr.at[i, rz])

    doc_forward(0)
    doc_forward(1)

    def project(w, n):
        return dot(w, gl[:, n * 256 : (n + 1) * 256])

    def g_last(n):
        for c in (2 * n, 2 * n + 1):
            g_wait(0, c)
            g_wait(2, c)

    def own(n):
        hgt[:, n * 256 : (n + 1) * 256] = project(wl[...], n)

    def partner(n, odd):
        rows = pl.ds(pl.multiple_of(lax.rem(x + odd, 2) * 256, 256), 256)
        cols = pl.ds(n * 256, 256)
        hs[rows, cols] = project(wp[rows, :], n).astype(BF16)
        send(hs.at[rows, cols], hr.at[rows, cols], hss.at[n, odd], hrs.at[n, odd], pdev)

    g_forward(0)
    for c in local[3:5]:
        c.wait()
    core_send(0)
    for rz in (1, 3):
        z_landed(rz)
        x_near(rz)
    g_forward(1)
    core_wait(0)
    pre_forward(0)
    x_pass(1)
    g_forward(2)
    w_spread(0)
    w_spread(1)
    w_core(0)
    x_pass(3)
    core_send(1)
    g_forward(3)
    core_wait(1)
    pre_forward(1)
    z_landed(2)
    x_near(2)
    g_last(0)
    for c in local[5:]:
        c.wait()
    w_wait(0)
    partner(0, 0)
    own(0)
    g_last(1)
    partner(1, 0)
    w_across()
    core_send(3)
    x_pass(2)
    w_wait(1)
    partner(0, 1)
    partner(1, 1)
    own(1)
    core_send(2)
    core_wait(3)
    pre_forward(3)
    core_wait(2)
    pre_forward(2)
    for hk in range(2):
        lanes = slice(hk * HD, (hk + 1) * HD)
        vv = vbuf[:, :, :, :, lanes].reshape(PRE, HD)
        ot[hk] = dot(vv, ebuf[hk].reshape(PRE, QW), ((0,), (0,))) + dot(vd[:, lanes], edoc[hk], ((0,), (0,)))
    for n in range(2):
        cols = pl.ds(n * 256, 256)
        for odd in range(2):
            rows = pl.ds(pl.multiple_of(lax.rem(x + odd, 2) * 256, 256), 256)
            landed(hr.at[rows, cols], hss.at[n, odd], hrs.at[n, odd])
        hgt[:, cols] += hr[:, cols].astype(F32)

    for hd in range(4):
        hk, cols = hd // 2, slice((hd % 2) * TOK, (hd % 2 + 1) * TOK)
        g = hgt[hd * HD : (hd + 1) * HD, :].astype(BF16).astype(F32)
        inv = 1.0 / jnp.sum(lsum[hk, :, cols], axis=0, keepdims=True)
        scaled = (g * inv).astype(BF16)
        drow[hk, :, cols] = jnp.sum(g * ot[hk, :, cols], axis=0, keepdims=True) * (inv * inv)
        dot_t[hk, :, cols] = scaled
        dos[hk, cols, :] = scaled.T

    def put_terms(a, hk, rz, t):
        t = t.astype(BF16).reshape(4, 2, 64, HD)
        for rc in range(2):
            pb[rz, a, rc, :, :, hk * HD : (hk + 1) * HD] = t[:, rc]

    def dv_block(rz):
        for hk in range(2):
            put_terms(0, hk, rz, dot(ebuf[hk, :, :, rz].reshape(QR, QW), dos[hk]))
        pair_send(rz, 0)

    def logit_grads(vv, hk, s, cols):
        dp = dot(vv, dot_t[hk, :, cols]) - drow[hk, :, cols]
        return (s.astype(F32) * dp).astype(BF16)

    def dk_block(rz):
        for hk in range(2):
            vv = vbuf[:, :, rz, :, hk * HD : (hk + 1) * HD].reshape(QR, HD)
            for n in range(2):
                cols = slice(n * TOK, (n + 1) * TOK)
                ds = logit_grads(vv, hk, sbuf[hk, :, :, rz, :, cols].reshape(QR, TOK), cols)
                sbuf[hk, :, :, rz, :, cols] = ds.reshape(4, 2, 64, TOK)
            put_terms(1, hk, rz, dot(sbuf[hk, :, :, rz].reshape(QR, QW), qs[hk]) * SCALE)
        pair_send(rz, 1)

    def pair_send(rz, a):
        send(pb.at[rz, a, 1], pr.at[rz, a], ps.at[rz, a], prs.at[rz, a], other)

    def pair_sum(rz, a, rx):
        return pb[rz, a, 0, rx].astype(F32) + pr[rz, a, rx].astype(F32)

    def x_send(rz, a):
        landed(pr.at[rz, a], ps.at[rz, a], prs.at[rz, a])
        for rx in (2, 1, 3):
            n = rx - 1
            xs[rz, a, n] = pair_sum(rz, a, rx).astype(BF16)
            send(xs.at[rz, a, n], xr.at[rz, a, n], xss.at[rz, a, n], xrs.at[rz, a, n], xdev[rx - 4])

    def x_total(rz):
        for a in range(2):
            t = pair_sum(rz, a, 0)
            for n in range(3):
                landed(xr.at[rz, a, n], xss.at[rz, a, n], xrs.at[rz, a, n])
                t = t + xr[rz, a, n].astype(F32)
            if rz:
                zs[rz - 1, a] = t.astype(BF16)
            else:
                tacc[a] = t
        if rz:
            send(zs.at[rz - 1], zr.at[rz - 1], zss.at[rz - 1], zrs.at[rz - 1], zdev[rz])

    outs = []

    def put(src, dst, n):
        c = pltpu.make_async_copy(src, dst, osem.at[n])
        c.start()
        outs.append(c)

    def z_in(n):
        landed(zr.at[n], zss.at[n], zrs.at[n])

    dv_block(2)
    dk_block(2)
    x_send(2, 0)
    dv_block(1)
    x_send(2, 1)
    dk_block(1)
    x_send(1, 0)
    dv_block(3)
    x_send(1, 1)
    dk_block(3)
    x_send(3, 0)
    dv_block(0)
    x_send(3, 1)
    dk_block(0)
    x_send(0, 0)
    x_total(2)

    def doc_backward(hk):
        lanes = slice(hk * HD, (hk + 1) * HD)
        for n in range(2):
            cols = slice(n * TOK, (n + 1) * TOK)
            sdoc[hk, :, cols] = logit_grads(vd[:, lanes], hk, sdoc[hk, :, cols], cols)
        odk[:, lanes] = (dot(sdoc[hk], qs[hk]) * SCALE).astype(BF16)
        odv[:, lanes] = dot(edoc[hk], dos[hk]).astype(BF16)

    doc_backward(0)
    x_send(0, 1)
    x_total(1)
    doc_backward(1)
    put(odk, dk_hbm, 2)
    put(odv, dv_hbm, 3)
    x_total(3)
    for hk in range(2):
        lanes = slice(hk * HD, (hk + 1) * HD)
        kk = kbuf[:, :, :, :, lanes].reshape(PRE, HD)
        t = dot(kk, sbuf[hk].reshape(PRE, QW), ((0,), (0,))) + dot(kd[:, lanes], sdoc[hk], ((0,), (0,)))
        for g in range(2):
            hd = hk * 2 + g
            odq[:, hd * HD : (hd + 1) * HD] = (t[:, g * TOK : (g + 1) * TOK] * SCALE).astype(BF16).T
    put(odq, dq_hbm, 4)
    x_total(0)
    for n in (1, 0, 2):
        z_in(n)
    for a, out, dst in ((0, opv, pdv_hbm), (1, opk, pdk_hbm)):
        out[...] = (tacc[a] + zr[0, a].astype(F32) + zr[1, a].astype(F32) + zr[2, a].astype(F32)).astype(BF16)
        put(out, dst, a)
    for c in started:
        c.wait_send()
    for c in outs:
        c.wait()


def finish(*refs):
    ins, outs, held, sem = refs[:5], refs[5:10], refs[10:15], refs[15]
    into = [pltpu.make_async_copy(a, b, sem.at[0, i]) for i, (a, b) in enumerate(zip(ins, held))]
    back = [pltpu.make_async_copy(a, b, sem.at[1, i]) for i, (a, b) in enumerate(zip(held, outs))]
    for c in into:
        c.start()
    for a, b in zip(into, back):
        a.wait()
        b.start()
    for c in back:
        c.wait()


def on_device(queries, keys, values, prefix_keys, prefix_values, out_grad, out_weight, doc_lengths):
    sd = jax.ShapeDtypeStruct
    hbm = pl.BlockSpec(memory_space=pl.ANY)
    vm = pltpu.VMEM
    dma = pltpu.SemaphoreType.DMA
    shapes = (
        sd((TOK, 512), BF16),
        sd((TOK, 256), BF16),
        sd((TOK, 256), BF16),
        sd((64, 256), BF16),
        sd((64, 256), BF16),
    )
    grads = pl.pallas_call(
        kernel,
        out_shape=shapes,
        in_specs=[pl.BlockSpec(memory_space=pltpu.SMEM)] + [hbm] * 7,
        out_specs=(hbm,) * 5,
        scratch_shapes=[
            vm((TOK, 512), BF16),
            vm((TOK, 256), BF16),
            vm((TOK, 256), BF16),
            vm((LAY, TOK), BF16),
            vm((512, LAY), BF16),
            vm((512, LAY), BF16),
            vm((512, TOK), BF16),
            vm((512, TOK), BF16),
            vm((4, 2, 4, 64, 256), BF16),
            vm((4, 2, 4, 64, 256), BF16),
            vm((2, 4, 2, 4, 64, QW), BF16),
            vm((2, 4, 2, 4, 64, QW), BF16),
            vm((2, TOK, QW), BF16),
            vm((2, TOK, QW), BF16),
            vm((2, HD, QW), BF16),
            vm((2, QW, HD), BF16),
            vm((2, HD, QW), BF16),
            vm((2, QW, HD), BF16),
            vm((2, HD, QW), F32),
            vm((2, 8, QW), F32),
            vm((2, 1, QW), F32),
            vm((512, TOK), F32),
            vm((4, 2, 2, 4, 64, 256), BF16),
            vm((4, 2, 4, 64, 256), BF16),
            vm((4, 2, 3, 64, 256), BF16),
            vm((4, 2, 3, 64, 256), BF16),
            vm((2, 64, 256), F32),
            vm((3, 2, 64, 256), BF16),
            vm((3, 2, 64, 256), BF16),
            vm((TOK, 512), BF16),
            vm((TOK, 256), BF16),
            vm((TOK, 256), BF16),
            vm((64, 256), BF16),
            vm((64, 256), BF16),
            dma((7,)),
            dma((3, NC)),
            dma((3, NC)),
            dma((2, 2)),
            dma((2, 2)),
            dma((2,)),
            dma((2,)),
            dma((2,)),
            dma((2,)),
            dma((2,)),
            dma((2,)),
            dma((2, 3)),
            dma((2, 3)),
            dma((2, 4, 3)),
            dma((2, 4, 3)),
            dma((2, 4)),
            dma((2, 4)),
            dma((4, 2)),
            dma((4, 2)),
            dma((4, 2, 3)),
            dma((4, 2, 3)),
            dma((3,)),
            dma((3,)),
            dma((5,)),
        ],
        compiler_params=pltpu.CompilerParams(
            collective_id=0, has_side_effects=True, vmem_limit_bytes=60 * 1024 * 1024
        ),
    )(doc_lengths, queries, keys, values, prefix_keys, prefix_values, out_grad.T, out_weight)
    return pl.pallas_call(
        finish,
        out_shape=shapes,
        in_specs=[hbm] * 5,
        out_specs=(hbm,) * 5,
        scratch_shapes=[vm(s.shape, s.dtype) for s in shapes] + [dma((2, 5))],
    )(*grads)


def solution(mesh):
    return jax.shard_map(
        on_device,
        mesh=mesh,
        in_specs=(P("docs", "heads"),) * 6 + (P("heads", None), P("docs", None)),
        out_specs=(P("docs", "heads"),) * 5,
        check_vma=False,
    )
```

time: 69.8 us -> 68 us (0.974)
  Pallas kernels: 68.4 us -> 67.1 us
    pallas_call x1, Pallas kernels: 66.2 us -> 65 us  [on_device(): pl.pallas_call(kernel, out_shape=shapes, in_specs=[pl.BlockSpec(memory_sp...]
where the time goes in v3:
time: 68 us; the launch traced here: 67.9 us
  Pallas kernels  67.1 us (99%)
  between operations  0.8 us (1%)
    pallas_call x1, Pallas kernels, on_device(): pl.pallas_call(kernel, out_shape=shapes, in_specs=[pl.BlockSpec(memory_sp...  65 us
    pallas_call x1, Pallas kernels, on_device(): pl.pallas_call(finish, out_shape=shapes, in_specs=[hbm] * 5, out_specs=(h...  2.1 us

profile of v3, /device:TPU:1, one launch (start us, length us, event | category | flops | bytes accessed | tf_op | source)
XLA Modules:
  0.0 67.9 jit_solution(6708207449293387170)
XLA Ops:
  0.6 65.0 %shard_map.119 = (bf16[512,512]{1,0:T(8,128)(2,1)}, bf16[512,256]{1,0:T(8,128)(2,1)}, bf16[512,256]{1,0:T(8,128)(2,1)}, bf16[64,256]{1,0:T(8,128)(2,1)}, bf16[64,256]{1,0:T(8,128)(2,1)}) custom-call(s32[1,3]{1,0:T(1,128)} %len_ref.1, bf16[512,512]{1,0:T(8,128)(2,1)} %q_hbm.1, bf16[512,256]{1,0:T(8,128)(2,1)} %k_hbm.1, bf16[512,256]{1,0:T(8,128)(2,1)} %v_hbm.1, ...), custom_call_target="tpu_custom_call" | custom-call | tf_op jit(solution)/shard_map/pallas_call | solution.py:459
  65.6 2.1 %shard_map.120 = (bf16[512,512]{1,0:T(8,128)(2,1)}, bf16[512,256]{1,0:T(8,128)(2,1)}, bf16[512,256]{1,0:T(8,128)(2,1)}, bf16[64,256]{1,0:T(8,128)(2,1)}, bf16[64,256]{1,0:T(8,128)(2,1)}) custom-call(bf16[512,512]{1,0:T(8,128)(2,1)} %get-tuple-element.10.refs_0_, bf16[512,256]{1,0:T(8,128)(2,1)} %get-tuple-element.11.refs_1_, ...), custom_call_target="tpu_custom_call" | custom-call | tf_op jit(solution)/shard_map/pallas_call | solution.py:528

commit v4 on v3

--- a/solution.py
+++ b/solution.py
@@ -31,8 +31,8 @@
     len_ref, q_hbm, k_hbm, v_hbm, pk_hbm, pv_hbm, og_hbm, w_hbm,
     dq_hbm, dk_hbm, dv_hbm, pdk_hbm, pdv_hbm,
     qb, kd, vd, gl, wl, wp, hs, hr, kbuf, vbuf, ebuf, sbuf, edoc, sdoc, qt, qs, dot_t, dos, ot, lsum, drow, hgt,
-    pb, pr, xs, xr, tacc, zs, zr, odq, odk, odv, opk, opv,
-    ls, gs, gr, hss, hrs, wzs, wzr, wxs, wxr, wcs, wcr, kzs, kzr, kxs, kxr, kcs, kcr, ps, prs, xss, xrs, zss, zrs, osem,
+    pb, pr, vs, vr, xs, xr, tacc, zs, zr, odq, odk, odv, opk, opv,
+    ls, gs, gr, hss, hrs, wzs, wzr, wcs, wcr, kzs, kzr, kxs, kxr, kcs, kcr, ps, prs, vss, vrs, xss, xrs, zss, zrs, osem,
 ):
     d = lax.axis_index("docs")
     h = lax.axis_index("heads")
@@ -113,45 +113,38 @@
         g_wait(1, c)
         g_send(2, c)
 
-    def w_rows(odd, rc, part):
-        first = lax.rem(x + odd, 2) * 256 + (core if rc == 0 else 1 - core) * 128
+    def w_rows(stage, rc, part):
+        first = stage * 256 + (core if rc == 0 else 1 - core) * 128
         if part is None:
             return pl.ds(pl.multiple_of(first, 128), 128)
         return pl.ds(pl.multiple_of(first + part * 64, 64), 64)
 
-    def w_send():
+    def w_send(stage):
         for part, to in ((0, pdev), (1, wdev)):
-            rows = w_rows(0, 0, part)
-            send(w_hbm.at[rows, layer(1 - zl)], wp.at[rows], wzs.at[part], wzr.at[part], to)
-
-    def w_spread(part):
-        rows = w_rows(0, 0, part)
-        landed(wp.at[rows], wzs.at[part], wzr.at[part])
-        send(wp.at[rows], wp.at[rows], wxs.at[part], wxr.at[part], xdev[1 - 2 * part])
-
-    def w_core(odd):
-        rows = w_rows(odd, 0, None)
-        send(wp.at[rows], wp.at[rows], wcs.at[odd], wcr.at[odd], other)
-
-    def w_across():
+            rows = w_rows(stage, 0, part)
+            send(w_hbm.at[rows, layer(1 - zl)], wp.at[rows], wzs.at[stage, part], wzr.at[stage, part], to)
+
+    def w_core(stage):
         for part in range(2):
-            landed(wp.at[w_rows(1, 0, part)], wxs.at[part], wxr.at[part])
-        w_core(1)
-
-    def w_wait(odd):
-        landed(wp.at[w_rows(odd, 1, None)], wcs.at[odd], wcr.at[odd])
+            landed(wp.at[w_rows(stage, 0, part)], wzs.at[stage, part], wzr.at[stage, part])
+        rows = w_rows(stage, 0, None)
+        send(wp.at[rows], wp.at[rows], wcs.at[stage], wcr.at[stage], other)
+
+    def w_wait(stage):
+        landed(wp.at[w_rows(stage, 1, None)], wcs.at[stage], wcr.at[stage])
 
     pre = ((0, kbuf, pk_hbm), (1, vbuf, pv_hbm))
     for i, buf, src in pre:
         send(src, buf.at[0, 0, 3], kzs.at[i, 2], kzr.at[i, 2], zdev[1])
         send(src, buf.at[0, 0, 1], kzs.at[i, 0], kzr.at[i, 0], zdev[3])
-    w_send()
+    w_send(0)
     for i, buf, src in pre:
         send(src, buf.at[0, 0, 2], kzs.at[i, 1], kzr.at[i, 1], zdev[2])
+    w_send(1)
     for i, buf, src in pre:
         for rx in (1, 3, 2):
             send(src, buf.at[rx, 0, 0], kxs.at[i, 0, rx - 1], kxr.at[i, 0, rx - 1], xdev[-rx])
-    for c in range(NC):
+    for c in range(3):
         g_send(0, c)
         g_send(1, c)
     for c in local[:3]:
@@ -251,11 +244,11 @@
     def own(n):
         hgt[:, n * 256 : (n + 1) * 256] = project(wl[...], n)
 
-    def partner(n, odd):
-        rows = pl.ds(pl.multiple_of(lax.rem(x + odd, 2) * 256, 256), 256)
+    def partner(n, stage):
+        rows = pl.ds(stage * 256, 256)
         cols = pl.ds(n * 256, 256)
         hs[rows, cols] = project(wp[rows, :], n).astype(BF16)
-        send(hs.at[rows, cols], hr.at[rows, cols], hss.at[n, odd], hrs.at[n, odd], pdev)
+        send(hs.at[rows, cols], hr.at[rows, cols], hss.at[n, stage], hrs.at[n, stage], pdev)
 
     g_forward(0)
     for c in local[3:5]:
@@ -265,38 +258,38 @@
         z_landed(rz)
         x_near(rz)
     g_forward(1)
+    g_send(0, 3)
+    g_send(1, 3)
     core_wait(0)
     pre_forward(0)
     x_pass(1)
+    x_pass(3)
     g_forward(2)
-    w_spread(0)
-    w_spread(1)
     w_core(0)
-    x_pass(3)
     core_send(1)
-    g_forward(3)
-    core_wait(1)
-    pre_forward(1)
-    z_landed(2)
-    x_near(2)
+    core_send(3)
     g_last(0)
     for c in local[5:]:
         c.wait()
     w_wait(0)
     partner(0, 0)
+    g_forward(3)
+    z_landed(2)
+    x_near(2)
+    core_wait(1)
+    pre_forward(1)
+    w_core(1)
     own(0)
+    x_pass(2)
     g_last(1)
     partner(1, 0)
-    w_across()
-    core_send(3)
-    x_pass(2)
     w_wait(1)
     partner(0, 1)
     partner(1, 1)
-    own(1)
     core_send(2)
     core_wait(3)
     pre_forward(3)
+    own(1)
     core_wait(2)
     pre_forward(2)
     for hk in range(2):
@@ -305,9 +298,9 @@
         ot[hk] = dot(vv, ebuf[hk].reshape(PRE, QW), ((0,), (0,))) + dot(vd[:, lanes], edoc[hk], ((0,), (0,)))
     for n in range(2):
         cols = pl.ds(n * 256, 256)
-        for odd in range(2):
-            rows = pl.ds(pl.multiple_of(lax.rem(x + odd, 2) * 256, 256), 256)
-            landed(hr.at[rows, cols], hss.at[n, odd], hrs.at[n, odd])
+        for stage in range(2):
+            rows = pl.ds(stage * 256, 256)
+            landed(hr.at[rows, cols], hss.at[n, stage], hrs.at[n, stage])
         hgt[:, cols] += hr[:, cols].astype(F32)
 
     for hd in range(4):
@@ -349,25 +342,41 @@
     def pair_sum(rz, a, rx):
         return pb[rz, a, 0, rx].astype(F32) + pr[rz, a, rx].astype(F32)
 
+    def pair_wait(rz, a):
+        landed(pr.at[rz, a], ps.at[rz, a], prs.at[rz, a])
+
+    def z_first(rz):
+        n = rz // 2
+        pair_wait(rz, 0)
+        for rx in range(4):
+            vs[n, rx] = pair_sum(rz, 0, rx).astype(BF16)
+        send(vs.at[n], vr.at[n], vss.at[n], vrs.at[n], zdev[rz])
+
+    def stay(a, rx):
+        t = pair_sum(0, a, rx)
+        return t if a else t + vr[0, rx].astype(F32) + vr[1, rx].astype(F32)
+
     def x_send(rz, a):
-        landed(pr.at[rz, a], ps.at[rz, a], prs.at[rz, a])
+        pair_wait(rz, a)
+        if rz == 0 and a == 0:
+            for n in range(2):
+                landed(vr.at[n], vss.at[n], vrs.at[n])
         for rx in (2, 1, 3):
             n = rx - 1
-            xs[rz, a, n] = pair_sum(rz, a, rx).astype(BF16)
+            t = pair_sum(rz, a, rx) if rz else stay(a, rx)
+            xs[rz, a, n] = t.astype(BF16)
             send(xs.at[rz, a, n], xr.at[rz, a, n], xss.at[rz, a, n], xrs.at[rz, a, n], xdev[rx - 4])
 
-    def x_total(rz):
-        for a in range(2):
-            t = pair_sum(rz, a, 0)
-            for n in range(3):
-                landed(xr.at[rz, a, n], xss.at[rz, a, n], xrs.at[rz, a, n])
-                t = t + xr[rz, a, n].astype(F32)
-            if rz:
-                zs[rz - 1, a] = t.astype(BF16)
-            else:
-                tacc[a] = t
+    def x_total(rz, a):
+        t = pair_sum(rz, a, 0) if rz else stay(a, 0)
+        for n in range(3):
+            landed(xr.at[rz, a, n], xss.at[rz, a, n], xrs.at[rz, a, n])
+            t = t + xr[rz, a, n].astype(F32)
         if rz:
-            send(zs.at[rz - 1], zr.at[rz - 1], zss.at[rz - 1], zrs.at[rz - 1], zdev[rz])
+            zs[rz - 1, a] = t.astype(BF16)
+            send(zs.at[rz - 1, a], zr.at[rz - 1, a], zss.at[rz - 1, a], zrs.at[rz - 1, a], zdev[rz])
+        else:
+            tacc[a] = t
 
     outs = []
 
@@ -376,25 +385,30 @@
         c.start()
         outs.append(c)
 
-    def z_in(n):
-        landed(zr.at[n], zss.at[n], zrs.at[n])
-
+    def z_total(a, out, dst):
+        t = tacc[a]
+        for n in (1, 0, 2) if a else (1,):
+            landed(zr.at[n, a], zss.at[n, a], zrs.at[n, a])
+            t = t + zr[n, a].astype(F32)
+        out[...] = t.astype(BF16)
+        put(out, dst, a)
+
+    dv_block(1)
+    dv_block(3)
     dv_block(2)
+    z_first(1)
     dk_block(2)
+    z_first(3)
     x_send(2, 0)
-    dv_block(1)
+    dk_block(1)
     x_send(2, 1)
-    dk_block(1)
-    x_send(1, 0)
-    dv_block(3)
+    dk_block(3)
     x_send(1, 1)
-    dk_block(3)
-    x_send(3, 0)
     dv_block(0)
     x_send(3, 1)
     dk_block(0)
-    x_send(0, 0)
-    x_total(2)
+    x_total(2, 0)
+    x_total(2, 1)
 
     def doc_backward(hk):
         lanes = slice(hk * HD, (hk + 1) * HD)
@@ -406,11 +420,13 @@
 
     doc_backward(0)
     x_send(0, 1)
-    x_total(1)
+    x_total(1, 1)
+    x_total(3, 1)
     doc_backward(1)
+    x_send(0, 0)
     put(odk, dk_hbm, 2)
     put(odv, dv_hbm, 3)
-    x_total(3)
+
     for hk in range(2):
         lanes = slice(hk * HD, (hk + 1) * HD)
         kk = kbuf[:, :, :, :, lanes].reshape(PRE, HD)
@@ -419,12 +435,10 @@
             hd = hk * 2 + g
             odq[:, hd * HD : (hd + 1) * HD] = (t[:, g * TOK : (g + 1) * TOK] * SCALE).astype(BF16).T
     put(odq, dq_hbm, 4)
-    x_total(0)
-    for n in (1, 0, 2):
-        z_in(n)
-    for a, out, dst in ((0, opv, pdv_hbm), (1, opk, pdk_hbm)):
-        out[...] = (tacc[a] + zr[0, a].astype(F32) + zr[1, a].astype(F32) + zr[2, a].astype(F32)).astype(BF16)
-        put(out, dst, a)
+    x_total(0, 1)
+    z_total(1, opk, pdk_hbm)
+    x_total(0, 0)
+    z_total(0, opv, pdv_hbm)
     for c in started:
         c.wait_send()
     for c in outs:
@@ -486,6 +500,8 @@
             vm((512, TOK), F32),
             vm((4, 2, 2, 4, 64, 256), BF16),
             vm((4, 2, 4, 64, 256), BF16),
+            vm((2, 4, 64, 256), BF16),
+            vm((2, 4, 64, 256), BF16),
             vm((4, 2, 3, 64, 256), BF16),
             vm((4, 2, 3, 64, 256), BF16),
             vm((2, 64, 256), F32),
@@ -501,10 +517,8 @@
             dma((3, NC)),
             dma((2, 2)),
             dma((2, 2)),
-            dma((2,)),
-            dma((2,)),
-            dma((2,)),
-            dma((2,)),
+            dma((2, 2)),
+            dma((2, 2)),
             dma((2,)),
             dma((2,)),
             dma((2, 3)),
@@ -515,10 +529,12 @@
             dma((2, 4)),
             dma((4, 2)),
             dma((4, 2)),
+            dma((2,)),
+            dma((2,)),
             dma((4, 2, 3)),
             dma((4, 2, 3)),
-            dma((3,)),
-            dma((3,)),
+            dma((3, 2)),
+            dma((3, 2)),
             dma((5,)),
         ],
         compiler_params=pltpu.CompilerParams(

time: 68 us -> 65 us (0.956)
  Pallas kernels: 67.1 us -> 64.1 us
    pallas_call x1, Pallas kernels: 65 us -> 62 us  [on_device(): pl.pallas_call(kernel, out_shape=shapes, in_specs=[pl.BlockSpec(memory_sp...]
where the time goes in v4:
time: 65 us; the launch traced here: 64.9 us
  Pallas kernels  64.1 us (99%)
  between operations  0.8 us (1%)
    pallas_call x1, Pallas kernels, on_device(): pl.pallas_call(kernel, out_shape=shapes, in_specs=[pl.BlockSpec(memory_sp...  62 us
    pallas_call x1, Pallas kernels, on_device(): pl.pallas_call(finish, out_shape=shapes, in_specs=[hbm] * 5, out_specs=(h...  2.1 us

profile of v4, /device:TPU:1, one launch (start us, length us, event | category | flops | bytes accessed | tf_op | source)
XLA Modules:
  0.0 64.9 jit_solution(2415006300239834043)
XLA Ops:
  0.6 62.0 %shard_map.119 = (bf16[512,512]{1,0:T(8,128)(2,1)}, bf16[512,256]{1,0:T(8,128)(2,1)}, bf16[512,256]{1,0:T(8,128)(2,1)}, bf16[64,256]{1,0:T(8,128)(2,1)}, bf16[64,256]{1,0:T(8,128)(2,1)}) custom-call(s32[1,3]{1,0:T(1,128)} %len_ref.1, bf16[512,512]{1,0:T(8,128)(2,1)} %q_hbm.1, bf16[512,256]{1,0:T(8,128)(2,1)} %k_hbm.1, bf16[512,256]{1,0:T(8,128)(2,1)} %v_hbm.1, ...), custom_call_target="tpu_custom_call" | custom-call | tf_op jit(solution)/shard_map/pallas_call | solution.py:473
  62.7 2.1 %shard_map.120 = (bf16[512,512]{1,0:T(8,128)(2,1)}, bf16[512,256]{1,0:T(8,128)(2,1)}, bf16[512,256]{1,0:T(8,128)(2,1)}, bf16[64,256]{1,0:T(8,128)(2,1)}, bf16[64,256]{1,0:T(8,128)(2,1)}) custom-call(bf16[512,512]{1,0:T(8,128)(2,1)} %get-tuple-element.10.refs_0_, bf16[512,256]{1,0:T(8,128)(2,1)} %get-tuple-element.11.refs_1_, ...), custom_call_target="tpu_custom_call" | custom-call | tf_op jit(solution)/shard_map/pallas_call | solution.py:544

commit v5 on v4

--- a/solution.py
+++ b/solution.py
@@ -138,9 +138,6 @@
         send(src, buf.at[0, 0, 3], kzs.at[i, 2], kzr.at[i, 2], zdev[1])
         send(src, buf.at[0, 0, 1], kzs.at[i, 0], kzr.at[i, 0], zdev[3])
     w_send(0)
-    for i, buf, src in pre:
-        send(src, buf.at[0, 0, 2], kzs.at[i, 1], kzr.at[i, 1], zdev[2])
-    w_send(1)
     for i, buf, src in pre:
         for rx in (1, 3, 2):
             send(src, buf.at[rx, 0, 0], kxs.at[i, 0, rx - 1], kxr.at[i, 0, rx - 1], xdev[-rx])
@@ -207,7 +204,7 @@
 
     def x_near(rz):
         for i, buf, _ in pre:
-            for rx in (1, 3):
+            for rx in (1, 3, 2) if rz == 2 else (1, 3):
                 send(buf.at[0, 0, rz], buf.at[rx, 0, rz], kxs.at[i, rz, rx - 1], kxr.at[i, rz, rx - 1], xdev[-rx])
 
     def x_landed(i, rx, rz):
@@ -222,7 +219,7 @@
     def core_send(rz):
         for i, buf, _ in pre:
             for rx in (1, 3, 2):
-                if rz == 0 or rx == 2 or rx == (1, 3)[i]:
+                if rz in (0, 2) or rx == 2 or rx == (1, 3)[i]:
                     x_landed(i, rx, rz)
             send(buf.at[:, 0, rz], buf.at[:, 1, rz], kcs.at[i, rz], kcr.at[i, rz], other)
 
@@ -256,6 +253,10 @@
     core_send(0)
     for rz in (1, 3):
         z_landed(rz)
+    for i, buf, _ in pre:
+        send(buf.at[0, 0, 3 - 2 * i], buf.at[0, 0, 2], kzs.at[i, 1], kzr.at[i, 1], zdev[1 + 2 * i])
+    w_send(1)
+    for rz in (1, 3):
         x_near(rz)
     g_forward(1)
     g_send(0, 3)
@@ -280,16 +281,15 @@
     pre_forward(1)
     w_core(1)
     own(0)
-    x_pass(2)
+    w_wait(1)
+    partner(0, 1)
     g_last(1)
     partner(1, 0)
-    w_wait(1)
-    partner(0, 1)
     partner(1, 1)
-    core_send(2)
     core_wait(3)
     pre_forward(3)
     own(1)
+    core_send(2)
     core_wait(2)
     pre_forward(2)
     for hk in range(2):
@@ -422,8 +422,8 @@
     x_send(0, 1)
     x_total(1, 1)
     x_total(3, 1)
+    x_send(0, 0)
     doc_backward(1)
-    x_send(0, 0)
     put(odk, dk_hbm, 2)
     put(odv, dv_hbm, 3)
 

time: 65 us -> 65.9 us (1.014)
  Pallas kernels: 64.1 us -> 65 us
    pallas_call x1, Pallas kernels: 62 us -> 62.9 us  [on_device(): pl.pallas_call(kernel, out_shape=shapes, in_specs=[pl.BlockSpec(memory_sp...]
where the time goes in v5:
time: 65.9 us; the launch traced here: 65.8 us
  Pallas kernels  65 us (99%)
  between operations  0.8 us (1%)
    pallas_call x1, Pallas kernels, on_device(): pl.pallas_call(kernel, out_shape=shapes, in_specs=[pl.BlockSpec(memory_sp...  62.9 us
    pallas_call x1, Pallas kernels, on_device(): pl.pallas_call(finish, out_shape=shapes, in_specs=[hbm] * 5, out_specs=(h...  2.1 us

profile of v5, /device:TPU:1, one launch (start us, length us, event | category | flops | bytes accessed | tf_op | source)
XLA Modules:
  0.0 65.8 jit_solution(1070539056380939245)
XLA Ops:
  0.6 62.9 %shard_map.119 = (bf16[512,512]{1,0:T(8,128)(2,1)}, bf16[512,256]{1,0:T(8,128)(2,1)}, bf16[512,256]{1,0:T(8,128)(2,1)}, bf16[64,256]{1,0:T(8,128)(2,1)}, bf16[64,256]{1,0:T(8,128)(2,1)}) custom-call(s32[1,3]{1,0:T(1,128)} %len_ref.1, bf16[512,512]{1,0:T(8,128)(2,1)} %q_hbm.1, bf16[512,256]{1,0:T(8,128)(2,1)} %k_hbm.1, bf16[512,256]{1,0:T(8,128)(2,1)} %v_hbm.1, ...), custom_call_target="tpu_custom_call" | custom-call | tf_op jit(solution)/shard_map/pallas_call | solution.py:473
  63.5 2.1 %shard_map.120 = (bf16[512,512]{1,0:T(8,128)(2,1)}, bf16[512,256]{1,0:T(8,128)(2,1)}, bf16[512,256]{1,0:T(8,128)(2,1)}, bf16[64,256]{1,0:T(8,128)(2,1)}, bf16[64,256]{1,0:T(8,128)(2,1)}) custom-call(bf16[512,512]{1,0:T(8,128)(2,1)} %get-tuple-element.10.refs_0_, bf16[512,256]{1,0:T(8,128)(2,1)} %get-tuple-element.11.refs_1_, ...), custom_call_target="tpu_custom_call" | custom-call | tf_op jit(solution)/shard_map/pallas_call | solution.py:544

commit v6 on v5

--- a/solution.py
+++ b/solution.py
@@ -277,19 +277,19 @@
     g_forward(3)
     z_landed(2)
     x_near(2)
+    own(0)
+    w_core(1)
     core_wait(1)
     pre_forward(1)
-    w_core(1)
-    own(0)
     w_wait(1)
     partner(0, 1)
     g_last(1)
     partner(1, 0)
     partner(1, 1)
+    core_send(2)
     core_wait(3)
     pre_forward(3)
     own(1)
-    core_send(2)
     core_wait(2)
     pre_forward(2)
     for hk in range(2):

time: 65.9 us -> 65.2 us (0.989)
  Pallas kernels: 65 us -> 64.3 us
where the time goes in v6:
time: 65.2 us; the launch traced here: 65.1 us
  Pallas kernels  64.3 us (99%)
  between operations  0.8 us (1%)
    pallas_call x1, Pallas kernels, on_device(): pl.pallas_call(kernel, out_shape=shapes, in_specs=[pl.BlockSpec(memory_sp...  62.2 us
    pallas_call x1, Pallas kernels, on_device(): pl.pallas_call(finish, out_shape=shapes, in_specs=[hbm] * 5, out_specs=(h...  2.1 us

profile of v6, /device:TPU:1, one launch (start us, length us, event | category | flops | bytes accessed | tf_op | source)
XLA Modules:
  0.0 65.1 jit_solution(1625641065881513584)
XLA Ops:
  0.6 62.2 %shard_map.119 = (bf16[512,512]{1,0:T(8,128)(2,1)}, bf16[512,256]{1,0:T(8,128)(2,1)}, bf16[512,256]{1,0:T(8,128)(2,1)}, bf16[64,256]{1,0:T(8,128)(2,1)}, bf16[64,256]{1,0:T(8,128)(2,1)}) custom-call(s32[1,3]{1,0:T(1,128)} %len_ref.1, bf16[512,512]{1,0:T(8,128)(2,1)} %q_hbm.1, bf16[512,256]{1,0:T(8,128)(2,1)} %k_hbm.1, bf16[512,256]{1,0:T(8,128)(2,1)} %v_hbm.1, ...), custom_call_target="tpu_custom_call" | custom-call | tf_op jit(solution)/shard_map/pallas_call | solution.py:473
  62.9 2.1 %shard_map.120 = (bf16[512,512]{1,0:T(8,128)(2,1)}, bf16[512,256]{1,0:T(8,128)(2,1)}, bf16[512,256]{1,0:T(8,128)(2,1)}, bf16[64,256]{1,0:T(8,128)(2,1)}, bf16[64,256]{1,0:T(8,128)(2,1)}) custom-call(bf16[512,512]{1,0:T(8,128)(2,1)} %get-tuple-element.10.refs_0_, bf16[512,256]{1,0:T(8,128)(2,1)} %get-tuple-element.11.refs_1_, ...), custom_call_target="tpu_custom_call" | custom-call | tf_op jit(solution)/shard_map/pallas_call | solution.py:544
